TPU v7x, 256 devices: a whole 4x4x8 slice. The times are simulated.
256 devices in a mesh: tile: 16 (over y, z_lo, core), seq: 16 (over x, z_hi).
Axes of the slice: x: 4, y: 4, z: 8 (z_hi: 4, z_lo: 2; z = z_hi * 2 + z_lo), core: 2. Of those that a mesh axis runs over, the one named last changes fastest.
Arguments:
- scene_band: bfloat16 [32, 1536, 768], P('seq', 'tile'), may hold values from -6 to 6
- tile_list: int32 [16, 3], replicated, may hold values from 0 to 32, as said below
- embed_weight: bfloat16 [768, 1024], replicated, may hold values from -0.21875 to 0.21875
- position: bfloat16 [2048, 1024], P('seq'), may hold values from -3 to 3
- norm_gains: float32 [3, 1024], replicated, may hold values from 0.1 to 1.9
- window_qkv: bfloat16 [1024, 3072], replicated
- window_out: bfloat16 [1024, 1024], replicated, may hold values from -0.1875 to 0.1875
- global_qkv: bfloat16 [1024, 3072], P(None, 'seq')
- global_out: bfloat16 [1024, 1024], P('seq')
- head_weight: bfloat16 [1024, 128], replicated, may hold values from -0.1875 to 0.1875
Outputs:
- strip_logits: float32 [32, 1536, 128], P('seq', 'tile')
Inputs may be any that keep to these rules, and one draw needn't show every extreme that they name: `tile_list`: column 0 is a tile's owning strip, 0 to 15; no strip owns more than 3 tiles and one strip owns exactly 3. Column 1 is the offset, 0 to 32, reached by some tile; column 2 the zero columns before the tile, 0 to 15, reached by some tile.
All inputs are finite; a program needn't handle non-finite values.
Results may differ from a plain program's by a relative error of at most 0.024.
Values may be sent and summed in bfloat16 or wider, within the bound.
A program may use at most 192 MiB of HBM per device.

v0:
```python
import jax
import jax.numpy as jnp
from jax import lax
from jax.sharding import PartitionSpec as P

D = 1024
H = 16
HD = 64
WIN = 16
PADMAX = 16
MOST = 3


EPSILON = 1e-06


def passed_along(array, axis, by):
    size = lax.axis_size(axis)
    pairs = [(i, i + by) for i in range(size) if 0 <= i + by < size]
    return lax.ppermute(array, axis, pairs)


def layer_norm(stream, gain):
    centre = stream - jnp.mean(stream, axis=-1, keepdims=True)
    spread = jnp.mean(centre * centre, axis=-1, keepdims=True)
    return (centre * lax.rsqrt(spread + EPSILON) * gain).astype(jnp.bfloat16)


def attend(queries, keys, values):
    scores = jnp.einsum("qhd,khd->hqk", queries, keys, preferred_element_type=jnp.float32) * HD ** (
        -0.5
    )
    weights = jax.nn.softmax(scores, axis=-1).astype(jnp.bfloat16)
    return jnp.einsum("hqk,khd->qhd", weights, values, preferred_element_type=jnp.float32).astype(
        jnp.bfloat16
    )


def global_attend(projected):
    token_count = projected.shape[0]
    local_heads = projected.shape[1] // (3 * HD)
    grouped = projected.reshape(token_count, local_heads, 3, HD)
    block_rows = min(512, token_count)
    queries = grouped[:, :, 0].reshape(token_count // block_rows, block_rows, local_heads, HD)
    keys = grouped[:, :, 1]
    values = grouped[:, :, 2]
    result = lax.map(lambda query_block: attend(query_block, keys, values), queries)
    return result.reshape(token_count, local_heads * HD)


def by_window(matrix, band_rows, tile_cols):
    width = matrix.shape[1]
    arranged = matrix.reshape(band_rows, tile_cols // WIN, WIN, width).transpose(1, 0, 2, 3)
    return arranged.reshape(tile_cols // WIN, band_rows * WIN, width)


def local(
    scene_band,
    tile_list,
    embed_weight,
    position,
    norm_gains,
    window_qkv,
    window_out,
    global_qkv,
    global_out,
    head_weight,
):
    tile_count = lax.axis_size("tile")
    my_tile = lax.axis_index("tile")
    band_rows, strip_cols, pixel_width = scene_band.shape
    tokens_here = position.shape[0]
    tile_cols = tokens_here // band_rows
    slab_cols = tile_cols // tile_count
    classes = head_weight.shape[1]
    owners = tile_list[:, 0]
    starts = tile_list[:, 1] - tile_list[:, 2] + PADMAX
    tile_ids = jnp.arange(tile_count, dtype=jnp.int32)
    shared = owners[:, None] == owners[None, :]
    earlier = tile_ids[None, :] < tile_ids[:, None]
    tile_rank = jnp.sum((shared & earlier).astype(jnp.int32), axis=1)
    slot_index = owners * MOST + tile_rank
    slot_ids = jnp.arange(tile_count * MOST, dtype=jnp.int32)
    matches = slot_index[None, :] == slot_ids[:, None]
    slot_used = jnp.any(matches, axis=1)
    slot_tile = jnp.sum(jnp.where(matches, tile_ids[None, :], 0), axis=1)
    own_tiles = lax.dynamic_slice_in_dim(slot_tile, my_tile * MOST, MOST)
    own_used = lax.dynamic_slice_in_dim(slot_used, my_tile * MOST, MOST)
    own_starts = starts[own_tiles]
    padded = jnp.concatenate(
        [jnp.zeros((band_rows, PADMAX, pixel_width), scene_band.dtype), scene_band], axis=1
    )

    def cut_block(start, used):
        block = lax.dynamic_slice_in_dim(padded, start, tile_cols, 1)
        return jnp.where(used, block, jnp.zeros_like(block))

    blocks = jax.vmap(cut_block)(own_starts, own_used)
    outgoing = blocks.reshape(MOST, band_rows, tile_count, slab_cols, pixel_width).transpose(
        2, 0, 1, 3, 4
    )
    arrived = lax.all_to_all(outgoing, "tile", split_axis=0, concat_axis=0, tiled=True)
    by_slot = arrived.reshape(tile_count * MOST, band_rows, slab_cols, pixel_width)
    forward = jnp.take(by_slot, slot_index, axis=0)
    collected = lax.all_to_all(forward, "tile", split_axis=0, concat_axis=0, tiled=True)
    pixels = collected.transpose(1, 0, 2, 3).reshape(tokens_here, pixel_width)
    stream = jnp.dot(pixels, embed_weight, preferred_element_type=jnp.float32) + position.astype(
        jnp.float32
    )
    normed = layer_norm(stream, norm_gains[0])
    projected = jnp.dot(normed, window_qkv, preferred_element_type=jnp.float32).astype(jnp.bfloat16)
    projected = projected.reshape(tokens_here, H, 3, HD)
    queries = projected[:, :, 0].reshape(tokens_here, D)
    own_pairs = projected[:, :, 1:].reshape(tokens_here, 2 * D)
    group_size = WIN // band_rows
    place = lax.axis_index("seq") % group_size
    pair_pieces = [own_pairs]
    piece_valid = [jnp.ones((), jnp.bool_)]
    for offset in range(1 - group_size, group_size):
        if offset == 0:
            continue
        piece = passed_along(own_pairs, "seq", offset)
        pair_pieces.append(piece)
        piece_valid.append((place - offset >= 0) & (place - offset < group_size))
    window_tokens = band_rows * WIN
    pairs = jnp.concatenate(
        [by_window(piece, band_rows, tile_cols) for piece in pair_pieces], axis=1
    )
    pairs = pairs.reshape(pairs.shape[0], pairs.shape[1], H, 2, HD)
    key_valid = jnp.repeat(jnp.stack(piece_valid), window_tokens)
    window_queries = by_window(queries, band_rows, tile_cols).reshape(
        tile_cols // WIN, window_tokens, H, HD
    )
    scores = jnp.einsum(
        "wqhd,wkhd->whqk", window_queries, pairs[:, :, :, 0], preferred_element_type=jnp.float32
    ) * HD ** (-0.5)
    scores = jnp.where(key_valid[None, None, None, :], scores, -jnp.inf)
    weights = jax.nn.softmax(scores, axis=-1).astype(jnp.bfloat16)
    mixed = jnp.einsum(
        "whqk,wkhd->wqhd", weights, pairs[:, :, :, 1], preferred_element_type=jnp.float32
    ).astype(jnp.bfloat16)
    mixed = (
        mixed.reshape(tile_cols // WIN, band_rows, WIN, D)
        .transpose(1, 0, 2, 3)
        .reshape(tokens_here, D)
    )
    stream = stream + jnp.dot(mixed, window_out, preferred_element_type=jnp.float32)
    normed = layer_norm(stream, norm_gains[1])
    features = lax.all_gather(normed, "seq", axis=0, tiled=True)
    projected = jnp.dot(features, global_qkv, preferred_element_type=jnp.float32).astype(
        jnp.bfloat16
    )
    attended = global_attend(projected)
    update = lax.psum_scatter(
        jnp.dot(attended, global_out, preferred_element_type=jnp.float32).astype(jnp.bfloat16),
        "seq",
        scatter_dimension=0,
        tiled=True,
    ).astype(jnp.float32)
    stream = stream + update
    logits = jnp.dot(
        layer_norm(stream, norm_gains[2]), head_weight, preferred_element_type=jnp.float32
    )
    outgoing_logits = logits.reshape(band_rows, tile_count, slab_cols, classes).transpose(
        1, 0, 2, 3
    )
    slabs = lax.all_to_all(
        outgoing_logits.astype(jnp.bfloat16), "tile", split_axis=0, concat_axis=0, tiled=True
    ).astype(outgoing_logits.dtype)
    held = jnp.take(slabs, slot_tile, axis=0) * slot_used.astype(jnp.float32)[:, None, None, None]
    held = held.reshape(tile_count, MOST, band_rows, slab_cols, classes)
    returned = lax.all_to_all(
        held.astype(jnp.bfloat16), "tile", split_axis=0, concat_axis=0, tiled=True
    ).astype(held.dtype)
    own_logits = returned.transpose(1, 2, 0, 3, 4).reshape(MOST, band_rows, tile_cols, classes)
    width_padded = PADMAX + strip_cols
    totals = jnp.zeros((band_rows, width_padded, classes), jnp.float32)
    coverage = jnp.zeros((width_padded,), jnp.float32)
    columns = jnp.arange(width_padded, dtype=jnp.int32)
    for member in range(MOST):
        start = own_starts[member]
        current = lax.dynamic_slice_in_dim(totals, start, tile_cols, 1)
        totals = lax.dynamic_update_slice_in_dim(totals, current + own_logits[member], start, 1)
        inside = (columns >= start) & (columns < start + tile_cols) & own_used[member]
        coverage = coverage + inside.astype(jnp.float32)
    return totals[:, PADMAX:] / jnp.maximum(coverage[PADMAX:], 1.0)[None, :, None]


def solution(mesh):
    return jax.shard_map(
        local,
        mesh=mesh,
        in_specs=(
            P("seq", "tile", None),
            P(),
            P(),
            P("seq", None),
            P(),
            P(),
            P(),
            P(None, "seq"),
            P("seq", None),
            P(),
        ),
        out_specs=P("seq", "tile", None),
        check_vma=False,
    )
```

profile of v0, /device:TPU:1, one launch (start us, length us, event | category | flops | bytes accessed | tf_op | source)
XLA Modules:
  0.0 674.0 jit_solution(9356330852032838798)
XLA Ops:
  14.0 7.3 %all-to-all-start = ((bf16[16,3,2,4,768]{4,3,2,1,0:T(4,128)(2,1)}), bf16[16,3,2,4,768]{4,3,2,1,0:T(4,128)(2,1)S(1)}, u32[]{:S(2)}, u32[]{:S(2)}) async-start(bf16[16,3,2,4,768]{4,3,2,1,0:T(4,128)(2,1)} %fusion.22), calls=%async_computation | async-start | bytes 1179648 | tf_op jit(solution)/shard_map/all_to_all | solution.py:102
  22.1 9.8 %all-to-all-done = bf16[16,3,2,4,768]{4,3,2,1,0:T(4,128)(2,1)S(1)} async-done(((bf16[16,3,2,4,768]{4,3,2,1,0:T(4,128)(2,1)}), bf16[16,3,2,4,768]{4,3,2,1,0:T(4,128)(2,1)S(1)}, u32[]{:S(2)}, u32[]{:S(2)}) %all-to-all-start) | async-done | bytes 589856 | tf_op jit(solution)/shard_map/all_to_all | solution.py:102
  33.5 4.5 all-to-all-start.1
  38.0 6.6 all-to-all-done.1
  46.9 4.8 convolution_convert_fusion.1
  62.4 31.5 %collective-permute-done = bf16[128,2048]{0,1:T(8,128)(2,1)} collective-permute-done((bf16[128,2048]{0,1:T(8,128)(2,1)}, bf16[128,2048]{0,1:T(8,128)(2,1)}, u32[]{:S(2)}, u32[]{:S(2)}) %collective-permute-start) | collective-permute-done | bytes 524320 | tf_op jit(solution)/shard_map/ppermute | solution.py:20
  99.5 19.7 %collective-permute-start.7 = (bf16[128,2048]{0,1:T(8,128)(2,1)}, bf16[128,2048]{0,1:T(8,128)(2,1)}, u32[]{:S(2)}, u32[]{:S(2)}) collective-permute-start(bf16[128,2048]{0,1:T(8,128)(2,1)} %bitcast.21), channel_id=1, source_target_pairs={{0,1},{1,2},{2,3},{3,4},{4,5},{5,6},{6,7},{7,8},{8,9},{9,10},{10,1... | collective-permute-start | bytes 1572872 | tf_op jit(solution)/shard_map/ppermute | solution.py:20
  119.2 8.2 %collective-permute-start.8 = (bf16[128,2048]{0,1:T(8,128)(2,1)}, bf16[128,2048]{0,1:T(8,128)(2,1)}, u32[]{:S(2)}, u32[]{:S(2)}) collective-permute-start(bf16[128,2048]{0,1:T(8,128)(2,1)} %bitcast.21), channel_id=1, source_target_pairs={{0,2},{1,3},{2,4},{3,5},{4,6},{5,7},{6,8},{7,9},{8,10},{9,11},{10,... | collective-permute-start | bytes 1572872 | tf_op jit(solution)/shard_map/ppermute | solution.py:20
  127.3 4.3 collective-permute-start.9
  131.7 20.4 %collective-permute-start.10 = (bf16[128,2048]{0,1:T(8,128)(2,1)}, bf16[128,2048]{0,1:T(8,128)(2,1)}, u32[]{:S(2)}, u32[]{:S(2)}) collective-permute-start(bf16[128,2048]{0,1:T(8,128)(2,1)} %bitcast.21), channel_id=1, source_target_pairs={{0,4},{1,5},{2,6},{3,7},{4,8},{5,9},{6,10},{7,11},{8,12},{9,13},{1... | collective-permute-start | bytes 1572872 | tf_op jit(solution)/shard_map/ppermute | solution.py:20
  152.1 29.7 %collective-permute-start.11 = (bf16[128,2048]{0,1:T(8,128)(2,1)}, bf16[128,2048]{0,1:T(8,128)(2,1)}, u32[]{:S(2)}, u32[]{:S(2)}) collective-permute-start(bf16[128,2048]{0,1:T(8,128)(2,1)} %bitcast.21), channel_id=1, source_target_pairs={{0,5},{1,6},{2,7},{3,8},{4,9},{5,10},{6,11},{7,12},{8,13},{9,14},{... | collective-permute-start | bytes 1572872 | tf_op jit(solution)/shard_map/ppermute | solution.py:20
  183.8 31.8 %collective-permute-start.13 = (bf16[128,2048]{0,1:T(8,128)(2,1)}, bf16[128,2048]{0,1:T(8,128)(2,1)}, u32[]{:S(2)}, u32[]{:S(2)}) collective-permute-start(bf16[128,2048]{0,1:T(8,128)(2,1)} %bitcast.21), channel_id=1, source_target_pairs={{0,7},{1,8},{2,9},{3,10},{4,11},{5,12},{6,13},{7,14},{8,15},{16,23... | collective-permute-start | bytes 1572872 | tf_op jit(solution)/shard_map/ppermute | solution.py:20
  228.1 4.2 copy.273
  242.6 4.2 copy.274
  254.2 4.2 copy.275
  265.9 4.2 copy.276
  277.5 4.1 copy.277
  289.0 4.2 copy.278
  312.0 4.2 copy.280
  324.0 4.2 copy.281
  335.5 4.2 copy.282
  347.1 4.1 copy.283
  358.6 4.2 copy.284
  370.2 4.2 copy.285
  381.9 4.2 copy.286
  393.4 4.1 copy.287
  397.6 30.2 %concatenate.57 = bf16[4,480,16,2,64]{1,4,2,0,3:T(8,128)(2,1)} concatenate(bf16[4,32,16,2,64]{1,4,2,0,3:T(8,128)(2,1)} %copy.273, bf16[4,32,16,2,64]{1,4,2,0,3:T(8,128)(2,1)} %copy.274, bf16[4,32,16,2,64]{1,4,2,0,3:T(8,128)(2,1)} %copy.275, bf16[4,32,16,2,64]{1,4,2,0,3:T(8,128)(2,1)} %copy.276, bf16[4,32,16,2,64]{1,4,2,0,3:T(8,128)(2,1)} %copy.277, ...), dimensions={1} | concatenate | bytes 15728640 | tf_op jit(solution)/shard_map/concatenate | solution.py:126
  437.8 85.4 %all-gather.2.cloned.1.call-done = bf16[2048,1024]{1,0:T(8,128)(2,1)} async-done(((bf16[128,1024]{1,0:T(8,128)(2,1)}), bf16[2048,1024]{1,0:T(8,128)(2,1)}) %all-gather.2.cloned.1.call-update) | async-done | bytes 4194320 | tf_op jit(solution)/shard_map/all_gather | solution.py:149
  527.3 11.3 %while.10 = (s32[]{:T(128)}, bf16[4,512,1,64]{1,3,2,0:T(8,128)(2,1)S(1)}, bf16[4,512,1,64]{1,3,2,0:T(8,128)(2,1)S(1)}, bf16[2048,1,64]{0,2,1:T(8,128)(2,1)S(1)}, bf16[2048,1,64]{0,2,1:T(8,128)(2,1)S(1)}, /*index=5*/s32[]{:T(128)}) while((s32[]{:T(128)}, bf16[4,512,1,64]{1,3,2,0:T(8,128)(2,1)S(1)}, bf16[4,512,1,64]{1,3,2,0:T(8,128)(2,1)S(1)}, ...), condition=%wide.region_12.13_spmd, body=%wide.region_9.12_spmd.sunk | while | flops 277904384 | bytes 13248589 | solution.py:47
  551.5 87.0 %reduce-scatter.2.cloned.1.call-done = bf16[128,1024]{1,0:T(8,128)(2,1)} async-done(((bf16[2048,1024]{1,0:T(8,128)(2,1)}), bf16[128,1024]{1,0:T(8,128)(2,1)}) %reduce-scatter.2.cloned.1.call-update) | async-done | bytes 262160 | tf_op jit(solution)/shard_map/reduce_scatter | solution.py:154
  642.6 5.6 all-to-all-start.2
  659.3 5.8 all-to-all-done.3
  (185 shorter events, 200.8 us)
Async XLA Ops:
  6.5 429.6 %copy-start = (bf16[1024,1024]{1,0:T(8,128)(2,1)S(1)}, bf16[1024,1024]{1,0:T(8,128)(2,1)}, u32[]{:S(2)}) copy-start(bf16[1024,1024]{1,0:T(8,128)(2,1)} %param.18) | copy-start | bytes 6291460
  6.5 31.4 %copy-start.6 = (f32[3,1024]{1,0:T(4,128)S(1)}, f32[3,1024]{1,0:T(4,128)}, u32[]{:S(2)}) copy-start(f32[3,1024]{1,0:T(4,128)} %param.16) | copy-start | bytes 36868
  6.5 38.2 %copy-start.4 = (bf16[128,1024]{1,0:T(8,128)(2,1)S(1)}, bf16[128,1024]{1,0:T(8,128)(2,1)}, u32[]{:S(2)}) copy-start(bf16[128,1024]{1,0:T(8,128)(2,1)} %param.15) | copy-start | bytes 786436
  14.0 17.9 %all-to-all-start = ((bf16[16,3,2,4,768]{4,3,2,1,0:T(4,128)(2,1)}), bf16[16,3,2,4,768]{4,3,2,1,0:T(4,128)(2,1)S(1)}, u32[]{:S(2)}, u32[]{:S(2)}) async-start(bf16[16,3,2,4,768]{4,3,2,1,0:T(4,128)(2,1)} %fusion.22), calls=%async_computation | async-start | bytes 1179648 | tf_op jit(solution)/shard_map/all_to_all | solution.py:102
  33.5 11.2 %all-to-all-start.1 = ((bf16[16,2,4,768]{3,2,1,0:T(4,128)(2,1)}), bf16[16,2,4,768]{3,2,1,0:T(4,128)(2,1)S(1)}, u32[]{:S(2)}, u32[]{:S(2)}) async-start(bf16[16,2,4,768]{3,2,1,0:T(4,128)(2,1)} %broadcast_select_fusion), calls=%async_computation.1 | async-start | bytes 393216 | tf_op jit(solution)/shard_map/all_to_all | solution.py:105
  37.9 485.3 %all-gather.2.cloned.1.call-start = ((), (), s32[]{:S(2)}) async-start(), calls=%async_computation.5 | async-start | bytes 4456448 | tf_op jit(solution)/shard_map/all_gather | solution.py:149
  55.9 38.0 %collective-permute-start = (bf16[128,2048]{0,1:T(8,128)(2,1)}, bf16[128,2048]{0,1:T(8,128)(2,1)}, u32[]{:S(2)}, u32[]{:S(2)}) collective-permute-start(bf16[128,2048]{0,1:T(8,128)(2,1)} %bitcast.21), channel_id=1, source_target_pairs={{7,0},{8,1},{9,2},{10,3},{11,4},{12,5},{13,6},{14,7},{15,8},{23,16... | collective-permute-start | bytes 1572872 | tf_op jit(solution)/shard_map/ppermute | solution.py:20
  57.2 38.0 %collective-permute-start.1 = (bf16[128,2048]{0,1:T(8,128)(2,1)}, bf16[128,2048]{0,1:T(8,128)(2,1)}, u32[]{:S(2)}, u32[]{:S(2)}) collective-permute-start(bf16[128,2048]{0,1:T(8,128)(2,1)} %bitcast.21), channel_id=1, source_target_pairs={{6,0},{7,1},{8,2},{9,3},{10,4},{11,5},{12,6},{13,7},{14,8},{15,9},... | collective-permute-start | bytes 1572872 | tf_op jit(solution)/shard_map/ppermute | solution.py:20
  58.5 41.0 %collective-permute-start.2 = (bf16[128,2048]{0,1:T(8,128)(2,1)}, bf16[128,2048]{0,1:T(8,128)(2,1)}, u32[]{:S(2)}, u32[]{:S(2)}) collective-permute-start(bf16[128,2048]{0,1:T(8,128)(2,1)} %bitcast.21), channel_id=1, source_target_pairs={{5,0},{6,1},{7,2},{8,3},{9,4},{10,5},{11,6},{12,7},{13,8},{14,9},{... | collective-permute-start | bytes 1572872 | tf_op jit(solution)/shard_map/ppermute | solution.py:20
  59.8 59.4 %collective-permute-start.3 = (bf16[128,2048]{0,1:T(8,128)(2,1)}, bf16[128,2048]{0,1:T(8,128)(2,1)}, u32[]{:S(2)}, u32[]{:S(2)}) collective-permute-start(bf16[128,2048]{0,1:T(8,128)(2,1)} %bitcast.21), channel_id=1, source_target_pairs={{4,0},{5,1},{6,2},{7,3},{8,4},{9,5},{10,6},{11,7},{12,8},{13,9},{1... | collective-permute-start | bytes 1572872 | tf_op jit(solution)/shard_map/ppermute | solution.py:20
  61.1 66.3 %collective-permute-start.4 = (bf16[128,2048]{0,1:T(8,128)(2,1)}, bf16[128,2048]{0,1:T(8,128)(2,1)}, u32[]{:S(2)}, u32[]{:S(2)}) collective-permute-start(bf16[128,2048]{0,1:T(8,128)(2,1)} %bitcast.21), channel_id=1, source_target_pairs={{3,0},{4,1},{5,2},{6,3},{7,4},{8,5},{9,6},{10,7},{11,8},{12,9},{13... | collective-permute-start | bytes 1572872 | tf_op jit(solution)/shard_map/ppermute | solution.py:20
  93.9 37.7 %collective-permute-start.5 = (bf16[128,2048]{0,1:T(8,128)(2,1)}, bf16[128,2048]{0,1:T(8,128)(2,1)}, u32[]{:S(2)}, u32[]{:S(2)}) collective-permute-start(bf16[128,2048]{0,1:T(8,128)(2,1)} %bitcast.21), channel_id=1, source_target_pairs={{2,0},{3,1},{4,2},{5,3},{6,4},{7,5},{8,6},{9,7},{10,8},{11,9},{12,... | collective-permute-start | bytes 1572872 | tf_op jit(solution)/shard_map/ppermute | solution.py:20
  95.2 56.9 %collective-permute-start.6 = (bf16[128,2048]{0,1:T(8,128)(2,1)}, bf16[128,2048]{0,1:T(8,128)(2,1)}, u32[]{:S(2)}, u32[]{:S(2)}) collective-permute-start(bf16[128,2048]{0,1:T(8,128)(2,1)} %bitcast.21), channel_id=1, source_target_pairs={{1,0},{2,1},{3,2},{4,3},{5,4},{6,5},{7,6},{8,7},{9,8},{10,9},{11,1... | collective-permute-start | bytes 1572872 | tf_op jit(solution)/shard_map/ppermute | solution.py:20
  99.5 82.3 %collective-permute-start.7 = (bf16[128,2048]{0,1:T(8,128)(2,1)}, bf16[128,2048]{0,1:T(8,128)(2,1)}, u32[]{:S(2)}, u32[]{:S(2)}) collective-permute-start(bf16[128,2048]{0,1:T(8,128)(2,1)} %bitcast.21), channel_id=1, source_target_pairs={{0,1},{1,2},{2,3},{3,4},{4,5},{5,6},{6,7},{7,8},{8,9},{9,10},{10,1... | collective-permute-start | bytes 1572872 | tf_op jit(solution)/shard_map/ppermute | solution.py:20
  119.2 64.7 %collective-permute-start.8 = (bf16[128,2048]{0,1:T(8,128)(2,1)}, bf16[128,2048]{0,1:T(8,128)(2,1)}, u32[]{:S(2)}, u32[]{:S(2)}) collective-permute-start(bf16[128,2048]{0,1:T(8,128)(2,1)} %bitcast.21), channel_id=1, source_target_pairs={{0,2},{1,3},{2,4},{3,5},{4,6},{5,7},{6,8},{7,9},{8,10},{9,11},{10,... | collective-permute-start | bytes 1572872 | tf_op jit(solution)/shard_map/ppermute | solution.py:20
  127.3 212.4 %collective-permute-start.9 = (bf16[128,2048]{0,1:T(8,128)(2,1)}, bf16[128,2048]{0,1:T(8,128)(2,1)}, u32[]{:S(2)}, u32[]{:S(2)}) collective-permute-start(bf16[128,2048]{0,1:T(8,128)(2,1)} %bitcast.21), channel_id=1, source_target_pairs={{0,3},{1,4},{2,5},{3,6},{4,7},{5,8},{6,9},{7,10},{8,11},{9,12},{10... | collective-permute-start | bytes 1572872 | tf_op jit(solution)/shard_map/ppermute | solution.py:20
  131.7 219.5 %collective-permute-start.10 = (bf16[128,2048]{0,1:T(8,128)(2,1)}, bf16[128,2048]{0,1:T(8,128)(2,1)}, u32[]{:S(2)}, u32[]{:S(2)}) collective-permute-start(bf16[128,2048]{0,1:T(8,128)(2,1)} %bitcast.21), channel_id=1, source_target_pairs={{0,4},{1,5},{2,6},{3,7},{4,8},{5,9},{6,10},{7,11},{8,12},{9,13},{1... | collective-permute-start | bytes 1572872 | tf_op jit(solution)/shard_map/ppermute | solution.py:20
  152.1 210.7 %collective-permute-start.11 = (bf16[128,2048]{0,1:T(8,128)(2,1)}, bf16[128,2048]{0,1:T(8,128)(2,1)}, u32[]{:S(2)}, u32[]{:S(2)}) collective-permute-start(bf16[128,2048]{0,1:T(8,128)(2,1)} %bitcast.21), channel_id=1, source_target_pairs={{0,5},{1,6},{2,7},{3,8},{4,9},{5,10},{6,11},{7,12},{8,13},{9,14},{... | collective-permute-start | bytes 1572872 | tf_op jit(solution)/shard_map/ppermute | solution.py:20
  181.8 192.6 %collective-permute-start.12 = (bf16[128,2048]{0,1:T(8,128)(2,1)}, bf16[128,2048]{0,1:T(8,128)(2,1)}, u32[]{:S(2)}, u32[]{:S(2)}) collective-permute-start(bf16[128,2048]{0,1:T(8,128)(2,1)} %bitcast.21), channel_id=1, source_target_pairs={{0,6},{1,7},{2,8},{3,9},{4,10},{5,11},{6,12},{7,13},{8,14},{9,15},... | collective-permute-start | bytes 1572872 | tf_op jit(solution)/shard_map/ppermute | solution.py:20
  183.8 202.2 %collective-permute-start.13 = (bf16[128,2048]{0,1:T(8,128)(2,1)}, bf16[128,2048]{0,1:T(8,128)(2,1)}, u32[]{:S(2)}, u32[]{:S(2)}) collective-permute-start(bf16[128,2048]{0,1:T(8,128)(2,1)} %bitcast.21), channel_id=1, source_target_pairs={{0,7},{1,8},{2,9},{3,10},{4,11},{5,12},{6,13},{7,14},{8,15},{16,23... | collective-permute-start | bytes 1572872 | tf_op jit(solution)/shard_map/ppermute | solution.py:20
  430.6 3.4 copy-start.2
  437.7 200.7 %reduce-scatter.2.cloned.1.call-start = ((), (), s32[]{:S(2)}) async-start(), calls=%async_computation.6 | async-start | bytes 4456448 | tf_op jit(solution)/shard_map/reduce_scatter | solution.py:154
  527.3 11.6 %copy-start.5 = (bf16[64,1024]{1,0:T(8,128)(2,1)S(1)}, bf16[64,1024]{1,0:T(8,128)(2,1)}, u32[]{:S(2)}) copy-start(bf16[64,1024]{1,0:T(8,128)(2,1)} %param.20) | copy-start | bytes 393220
  539.0 101.7 %copy-start.3 = (bf16[1024,128]{1,0:T(8,128)(2,1)S(1)}, bf16[1024,128]{1,0:T(8,128)(2,1)}, u32[]{:S(2)}) copy-start(bf16[1024,128]{1,0:T(8,128)(2,1)} %param.21) | copy-start | bytes 786436
  542.2 124.7 %copy-start.1 = (bf16[1024,1024]{1,0:T(8,128)(2,1)S(1)}, bf16[1024,1024]{1,0:T(8,128)(2,1)}, u32[]{:S(2)}) copy-start(bf16[1024,1024]{1,0:T(8,128)(2,1)} %param.18) | copy-start | bytes 6291460
  642.6 11.4 %all-to-all-start.2 = ((bf16[16,2,4,128]{3,2,1,0:T(4,128)(2,1)}), bf16[16,2,4,128]{3,2,1,0:T(4,128)(2,1)S(1)}, u32[]{:S(2)}, u32[]{:S(2)}) async-start(bf16[16,2,4,128]{3,2,1,0:T(4,128)(2,1)} %bitcast.204), calls=%async_computation.3 | async-start | bytes 65536 | tf_op jit(solution)/shard_map/all_to_all | solution.py:167
  655.5 9.6 %all-to-all-start.3 = ((bf16[16,3,2,4,128]{4,3,2,1,0:T(4,128)(2,1)}), bf16[16,3,2,4,128]{4,3,2,1,0:T(4,128)(2,1)S(1)}, u32[]{:S(2)}, u32[]{:S(2)}) async-start(bf16[16,3,2,4,128]{4,3,2,1,0:T(4,128)(2,1)} %multiply_convert_fusion.5), calls=%async_computation.4 | async-start | bytes 196608 | tf_op jit(solution)/shard_map/all_to_all | solution.py:172
Sparse Core Ops, SparseCore 0:
  437.9 85.3 all-gather.1
  542.3 96.0 reduce-scatter.1
where the time goes:
time: 686 us; the launch traced here: 674 us
  waiting for transfers between devices  231 us (34%)
  local copies, waits for them, and re-layouts  228 us (33%)
  starting transfers between devices  146 us (21%)
  matrix products  27.5 us (4%)
  between operations  22 us (3%)
  other arithmetic  18.5 us (3%)
    concatenate x31, local copies, waits for them, and re-layouts, local(): jnp.concatenate([by_window(piece, band_rows, tile_cols) for piece in pair...  145 us
    ppermute x14, starting transfers between devices, passed_along(): return lax.ppermute(array, axis, pairs)  125 us
    reduce_scatter x1, waiting for transfers between devices, local(): lax.psum_scatter(jnp.dot(attended, global_out, preferred_element_type=jnp...  87 us
    all_gather x1, waiting for transfers between devices, local(): features = lax.all_gather(normed, 'seq', axis=0, tiled=True)  85.4 us
    ppermute x14, waiting for transfers between devices, passed_along(): return lax.ppermute(array, axis, pairs)  34.6 us
    ppermute x14, local copies, waits for them, and re-layouts, passed_along(): return lax.ppermute(array, axis, pairs)  28.5 us
    transpose x16, local copies, waits for them, and re-layouts, by_window(): matrix.reshape(band_rows, tile_cols // WIN, WIN, width)  28.1 us
  transfers between devices with their start and end apart: 20, of which 8 were waited for; matrix products, arithmetic and copies ran while one was open for 26% of the time, Pallas kernels for 0%

commit v1 on v0

v1 whole, which is shorter than its diff:
```python
import functools
import jax
import jax.numpy as jnp
from jax import lax
from jax.experimental import pallas as pl
from jax.experimental.pallas import tpu as pltpu
from jax.sharding import PartitionSpec as P

D = 1024
HD = 64
PADMAX = 16
MOST = 3
N = 16
SC = 96
PV = 768
FH = 384
NCLS = 128
EPSILON = 1e-06
FAR = 4096
NT = (((1,), (1,)), ((), ()))


def layer_norm(stream, gain):
    centre = stream - jnp.mean(stream, axis=-1, keepdims=True)
    spread = jnp.mean(centre * centre, axis=-1, keepdims=True)
    return (centre * lax.rsqrt(spread + EPSILON) * gain).astype(jnp.bfloat16)


def dot(a, b):
    return jnp.dot(a, b, preferred_element_type=jnp.float32)


def remote(src, dst, send_sem, recv_sem, tile, seq):
    return pltpu.make_async_remote_copy(
        src_ref=src, dst_ref=dst, send_sem=send_sem, recv_sem=recv_sem,
        device_id=(tile, seq), device_id_type=pl.DeviceIdType.MESH,
    )


def loop(low, high, body):
    def step(k, carry):
        body(k)
        return carry

    lax.fori_loop(low, high, step, 0)


def kernel(
    tl, strip, pos, wq, wo, gains, we_hbm, w1_hbm, wout_hbm, hw_hbm, out_ref,
    we, w1, wout, hw, load_sem,
    out1, in1, fwd, pix, posall, nbuf, x_ref, o1,
    wqall, woall, q_out, q_in, qt, kb, vt, o_out, o_in,
    lout, lin, rout, rin,
    entered,
    p1s, p1r, p2s, p2r, pos_s, pos_r, sib_s, sib_r,
    qzs, qxs, qss, qr, qsr, ozs, oxs, oss, orr, osr,
    as_, ar, bs, br, l1s, l1r, l2s, l2r,
):
    i = lax.axis_index("tile")
    r = lax.axis_index("seq")
    core = i % 2
    sibling = i + 1 - 2 * core
    x_at = r // 4
    z_at = r % 4
    band = i // 4
    upper = (i % 4) // 2
    kc_mine = 2 * band + core
    r8 = r // 8
    rm = r % 8

    loads = [
        pltpu.make_async_copy(we_hbm, we, load_sem.at[0]),
        pltpu.make_async_copy(w1_hbm, w1, load_sem.at[1]),
        pltpu.make_async_copy(wout_hbm, wout, load_sem.at[2]),
        pltpu.make_async_copy(hw_hbm, hw, load_sem.at[3]),
    ]
    for load in loads:
        load.start()

    barrier = pltpu.get_barrier_semaphore()

    def greet(k):
        pl.semaphore_signal(
            barrier, inc=1, device_id=((i + k) % N, r), device_id_type=pl.DeviceIdType.MESH
        )
        pl.semaphore_signal(
            barrier, inc=1, device_id=(i, (r + k) % N), device_id_type=pl.DeviceIdType.MESH
        )

    loop(1, N, greet)

    owners = [tl[t, 0] for t in range(N)]
    starts = [tl[t, 1] - tl[t, 2] for t in range(N)]
    ranks = []
    for t in range(N):
        rank = jnp.int32(0)
        for u in range(t):
            rank = rank + jnp.where(owners[u] == owners[t], 1, 0)
        ranks.append(jnp.minimum(rank, MOST - 1))
    begin = []
    for m in range(MOST):
        value = jnp.int32(FAR)
        for t in range(N):
            value = jnp.where((owners[t] == i) & (ranks[t] == m), starts[t], value)
        begin.append(value)

    cells = strip[...].reshape(2 * SC, PV)
    token = lax.broadcasted_iota(jnp.int32, (128, 2 * SC), 0)
    cell = lax.broadcasted_iota(jnp.int32, (128, 2 * SC), 1)
    t_row = (token // 8) % 2
    t_col = (token // 16) * 8 + token % 8
    c_row = jnp.where(cell >= SC, 1, 0)
    c_col = cell - SC * c_row
    for m in range(MOST):
        chosen = (c_row == t_row) & (c_col == t_col + begin[m])
        block = dot(jnp.where(chosen, 1.0, 0.0).astype(jnp.bfloat16), cells).astype(jnp.bfloat16)
        for c in range(N):
            k, f = c // 2, c % 2
            out1[c, m] = block[k * 16 : k * 16 + 16, f * FH : f * FH + FH]

    pl.semaphore_wait(barrier, 2 * (N - 1))

    def p1(c):
        return remote(out1.at[c], in1.at[i], p1s.at[c], p1r.at[i], c, r)

    def p1_in(s):
        return remote(out1.at[s], in1.at[s], p1s.at[s], p1r.at[s], s, r)

    loop(1, N, lambda k: p1((i + k) % N).start())
    in1[i] = out1[i]

    def greet_again(k):
        pl.semaphore_signal(
            entered, inc=1, device_id=(i, (r + k) % N), device_id_type=pl.DeviceIdType.MESH
        )

    loop(1, N, greet_again)

    def pos_copy(t):
        return remote(pos, posall.at[rm], pos_s.at[t], pos_r.at[rm], i, t)

    @pl.when(upper == r8)
    def _():
        loop(1, N, lambda k: pos_copy((r + k) % N).start())
        posall[rm] = pos[...]

    def along_z(src, full, zs, got, k):
        return remote(
            src.at[core], full.at[r, core], zs.at[k - 1], got.at[r], i, x_at * 4 + (z_at + k) % 4
        )

    def along_x(src, full, xs, got, z, k):
        shard = x_at * 4 + z
        piece = src.at[core] if src is not None else full.at[shard, core]
        return remote(
            piece, full.at[shard, core], xs.at[z * 3 + k - 1], got.at[shard],
            i, ((x_at + k) % 4) * 4 + z_at,
        )

    def arrival(src, full, zs, got, shard):
        return remote(src.at[core], full.at[shard, core], zs.at[0], got.at[shard], i, r)

    def to_sibling(full, ss, got, shard):
        return remote(
            full.at[shard, core], full.at[shard, core], ss.at[shard], got.at[shard], sibling, r
        )

    def from_sibling(full, ss, got, shard):
        return remote(
            full.at[shard, 1 - core], full.at[shard, 1 - core], ss.at[shard], got.at[shard],
            sibling, r,
        )

    def spread_own(src, full, zs, xs, got):
        for k in range(1, 4):
            along_z(src, full, zs, got, k).start()
        for k in range(1, 4):
            along_x(src, full, xs, got, z_at, k).start()
        full[r] = src[...]

    def pass_z(src, full, zs, xs, ss, got, sgot):
        def one(k):
            z = (z_at + k) % 4
            arrival(src, full, zs, got, x_at * 4 + z).wait_recv()
            for d in range(1, 4):
                along_x(None, full, xs, got, z, d).start()
            to_sibling(full, ss, sgot, x_at * 4 + z).start()

        loop(1, 4, one)

    def pass_x(src, full, zs, ss, got, sgot, k):
        z = (z_at + k) % 4
        for d in range(1, 4):
            shard = ((x_at + d) % 4) * 4 + z
            arrival(src, full, zs, got, shard).wait_recv()
            to_sibling(full, ss, sgot, shard).start()

    def finish_sends(src, full, zs, xs, ss, got, sgot):
        for k in range(1, 4):
            along_z(src, full, zs, got, k).wait_send()
        for k in range(0, 4):
            for d in range(1, 4):
                along_x(None, full, xs, got, (z_at + k) % 4, d).wait_send()

        loop(1, N, lambda k: to_sibling(full, ss, sgot, (r + k) % N).wait_send())

    spread_own(wq, wqall, qzs, qxs, qr)

    loop(1, N, lambda k: p1_in((i + k) % N).wait_recv())
    for t in range(N):
        fwd[t] = in1[owners[t], ranks[t]]
    pl.semaphore_wait(entered, N - 1)

    half_c = (i % 4) // 2
    worker = band * 4 + r8 * 2 + half_c

    def p2(t):
        return remote(
            fwd.at[t], pix.at[core, rm], p2s.at[t], p2r.at[core * 8 + rm], worker, t
        )

    loop(1, N, lambda k: p2((r + k) % N).start())

    @pl.when(worker != i)
    def _():
        p2(r).start()

    @pl.when(worker == i)
    def _():
        pix[core, rm] = fwd[r]

    pass_z(wq, wqall, qzs, qxs, qss, qr, qsr)

    for f in range(2):
        source = band * 4 + core * 2 + f

        def p2_in(k, f=f, source=source):
            @pl.when((source != i) | (upper * 8 + k != r))
            def _():
                remote(
                    fwd.at[0], pix.at[f, k], p2s.at[0], p2r.at[f * 8 + k], i, r
                ).wait_recv()

        loop(0, 8, p2_in)

    def pos_in(k):
        @pl.when(upper * 8 + k != r)
        def _():
            remote(pos, posall.at[k], pos_s.at[0], pos_r.at[k], i, r).wait_recv()

    loop(0, 8, pos_in)
    loads[0].wait()
    stream = dot(pix[0].reshape(128, FH), we[0:FH]) + dot(pix[1].reshape(128, FH), we[FH:PV])
    stream = stream + posall[...].reshape(128, D).astype(jnp.float32)
    x_ref[...] = stream
    nbuf[core] = layer_norm(stream, gains[0:1])
    sib = remote(nbuf.at[core], nbuf.at[core], sib_s, sib_r, sibling, r)
    sib.start()
    sib_in = remote(nbuf.at[1 - core], nbuf.at[1 - core], sib_s, sib_r, sibling, r)
    loads[1].wait()
    sib_in.wait_recv()

    def window_heads(pair):
        columns = w1[:, pl.ds(pl.multiple_of(pair * 384, 384), 384)]
        mine = dot(nbuf[core], columns).astype(jnp.bfloat16)
        other = dot(nbuf[1 - core], columns).astype(jnp.bfloat16)
        both = jnp.concatenate([mine, other], axis=0)
        results = []
        for h in range(2):
            at = h * 192
            scores = lax.dot_general(
                mine[:, at : at + 64], both[:, at + 64 : at + 128], NT,
                preferred_element_type=jnp.float32,
            ) * HD ** (-0.5)
            top = jnp.max(scores, axis=-1, keepdims=True)
            weights = jnp.exp(scores - top)
            weights = weights / jnp.sum(weights, axis=-1, keepdims=True)
            results.append(dot(weights.astype(jnp.bfloat16), both[:, at + 128 : at + 192]))
        o1[:, pl.ds(pl.multiple_of(pair * 128, 128), 128)] = jnp.concatenate(
            results, axis=1
        ).astype(jnp.bfloat16)

    loop(0, 4, window_heads)
    pass_x(wq, wqall, qzs, qss, qr, qsr, 0)
    loop(4, 8, window_heads)
    loads[2].wait()
    stream = x_ref[...] + dot(o1[...], wout[...])
    x_ref[...] = stream
    normed = layer_norm(stream, gains[1:2])
    for k in range(1, 4):
        pass_x(wq, wqall, qzs, qss, qr, qsr, k)
    loop(1, N, lambda k: from_sibling(wqall, qss, qsr, (r + k) % N).wait_recv())

    def to_head(h):
        return remote(q_out.at[h], q_in.at[i], as_.at[h], ar.at[i], h, r)

    def project(k):
        h = (i + k) % N
        q_out[h] = lax.dot_general(
            wqall[h].reshape(192, D), normed, NT, preferred_element_type=jnp.float32
        ).astype(jnp.bfloat16)
        to_head(h).start()

    loop(1, N, project)
    q_in[i] = lax.dot_general(
        wqall[i].reshape(192, D), normed, NT, preferred_element_type=jnp.float32
    ).astype(jnp.bfloat16)

    spread_own(wo, woall, ozs, oxs, orr)

    def head_in(k):
        s = (i + k) % N
        remote(q_out.at[s], q_in.at[s], as_.at[s], ar.at[s], s, r).wait_recv()

    loop(1, N, head_in)
    for s in range(N):
        at = s * 128
        qt[:, at : at + 128] = q_in[s, 0:64]
        kb[at : at + 128, :] = q_in[s, 64:128].astype(jnp.float32).T.astype(jnp.bfloat16)
        vt[:, at : at + 128] = q_in[s, 128:192]

    def home(j):
        return remote(o_out.at[j], o_in.at[i], bs.at[j], br.at[i], j, r)

    def attend(k):
        b = (k + i // 2 + 1) % 8
        queries = qt[:, pl.ds(pl.multiple_of(b * 256, 256), 256)]
        scores = dot(kb[...], queries)
        top = jnp.max(scores, axis=0, keepdims=True)
        weights = jnp.exp2((scores - top) * (HD ** (-0.5) * 1.4426950408889634))
        total = jnp.sum(weights, axis=0, keepdims=True)
        mixed = (dot(vt[...], weights.astype(jnp.bfloat16)) / total).astype(jnp.bfloat16)
        o_out[2 * b] = mixed[:, 0:128]
        o_out[2 * b + 1] = mixed[:, 128:256]
        for e in range(2):
            j = 2 * b + e

            @pl.when(j != i)
            def _(j=j):
                home(j).start()

    loop(0, 2, attend)
    pass_z(wo, woall, ozs, oxs, oss, orr, osr)
    loop(2, 7, attend)
    for k in range(0, 4):
        pass_x(wo, woall, ozs, oss, orr, osr, k)
    loop(7, 8, attend)
    o_in[i] = o_out[i]
    loop(1, N, lambda k: from_sibling(woall, oss, osr, (r + k) % N).wait_recv())

    def home_in(k):
        s = (i + k) % N
        remote(o_out.at[s], o_in.at[s], bs.at[s], br.at[s], s, r).wait_recv()

    loop(1, N, home_in)
    attended = o_in[...].reshape(D, 128).astype(jnp.float32).T.astype(jnp.bfloat16)
    stream = x_ref[...] + dot(attended, woall[...].reshape(D, D))
    loads[3].wait()
    logits = dot(layer_norm(stream, gains[2:3]), hw[...])
    lout[...] = logits.astype(jnp.bfloat16).reshape(8, 16, NCLS)

    collector = 2 * kc_mine + r % 2

    def l1(k):
        return remote(
            lout.at[k], lin.at[r // 2], l1s.at[k], l1r.at[r // 2], collector, upper * 8 + k
        )

    def l1_start(k):
        away = (collector != i) | (upper * 8 + k != r)

        @pl.when(away)
        def _():
            l1(k).start()

        @pl.when(jnp.logical_not(away))
        def _():
            lin[r // 2] = lout[k]

    loop(0, 8, l1_start)
    kc = i // 2
    giver = (kc // 2) * 4 + r8 * 2 + kc % 2

    def l1_in(k):
        @pl.when((giver != i) | (2 * k + i % 2 != r))
        def _():
            remote(lout.at[0], lin.at[k], l1s.at[0], l1r.at[k], i, r).wait_recv()

    slot = [owners[t] * MOST + ranks[t] for t in range(N)]
    lane = lax.broadcasted_iota(jnp.int32, (N * MOST * 16, 128), 1)
    line = lax.broadcasted_iota(jnp.int32, (N * MOST * 16, 128), 0)
    wanted = jnp.zeros((N * MOST * 16, 128), jnp.int32)
    for k in range(8):
        wanted = jnp.where(
            lane // 16 == k, jnp.where(core == 0, slot[2 * k], slot[2 * k + 1]), wanted
        )
    route = jnp.where(line == wanted * 16 + lane % 16, 1.0, 0.0).astype(jnp.bfloat16)
    loop(0, 8, l1_in)
    rout[...] = (
        dot(route, lin[...].reshape(128, NCLS)).astype(jnp.bfloat16).reshape(N, MOST, 16, NCLS)
    )

    def l2(s):
        return remote(rout.at[s], rin.at[i], l2s.at[s], l2r.at[i], s, r)

    loop(1, N, lambda k: l2((i + k) % N).start())
    rin[i] = rout[i]

    cell = lax.broadcasted_iota(jnp.int32, (2 * SC, 128), 0)
    token = lax.broadcasted_iota(jnp.int32, (2 * SC, 128), 1)
    t_row = (token // 8) % 2
    t_col = (token // 16) * 8 + token % 8
    c_row = jnp.where(cell >= SC, 1, 0)
    c_col = cell - SC * c_row
    count = jnp.zeros((2 * SC, 128), jnp.float32)
    spots = []
    for m in range(MOST):
        chosen = (c_row == t_row) & (c_col == t_col + begin[m])
        spots.append(jnp.where(chosen, 1.0, 0.0).astype(jnp.bfloat16))
        count = count + jnp.where((c_col >= begin[m]) & (c_col < begin[m] + 64), 1.0, 0.0)

    def l2_in(k):
        s = (i + k) % N
        remote(rout.at[s], rin.at[s], l2s.at[s], l2r.at[s], s, r).wait_recv()

    loop(1, N, l2_in)
    total = jnp.zeros((2 * SC, NCLS), jnp.float32)
    for m in range(MOST):
        pieces = [rin[2 * k, m] + rin[2 * k + 1, m] for k in range(8)]
        total = total + dot(spots[m], jnp.concatenate(pieces, axis=0))
    out_ref[...] = (total / jnp.maximum(count, 1.0)).reshape(2, SC, NCLS)

    loop(1, N, lambda k: p1((i + k) % N).wait_send())

    @pl.when(upper == r8)
    def _():
        loop(1, N, lambda k: pos_copy((r + k) % N).wait_send())

    loop(1, N, lambda k: p2((r + k) % N).wait_send())

    @pl.when(worker != i)
    def _():
        p2(r).wait_send()

    sib.wait_send()
    finish_sends(wq, wqall, qzs, qxs, qss, qr, qsr)
    finish_sends(wo, woall, ozs, oxs, oss, orr, osr)
    loop(1, N, lambda k: to_head((i + k) % N).wait_send())
    loop(1, N, lambda k: home((i + k) % N).wait_send())

    def l1_sent(k):
        @pl.when((collector != i) | (upper * 8 + k != r))
        def _():
            l1(k).wait_send()

    loop(0, 8, l1_sent)
    loop(1, N, lambda k: l2((i + k) % N).wait_send())


def local(
    scene_band, tile_list, embed_weight, position, norm_gains, window_qkv, window_out,
    global_qkv, global_out, head_weight,
):
    i = lax.axis_index("tile")
    column = 2 * (i // 4) + i % 2
    pos = lax.dynamic_slice_in_dim(position.reshape(2, 64, D), column * 8, 8, 1).reshape(16, D)
    wq = global_qkv.T.reshape(2, 96, D)
    wo = global_out.reshape(2, 32, D)
    bf = jnp.bfloat16
    vmem = pl.BlockSpec(memory_space=pltpu.VMEM)
    hbm = pl.BlockSpec(memory_space=pl.ANY)
    dma = pltpu.SemaphoreType.DMA
    return pl.pallas_call(
        kernel,
        out_shape=jax.ShapeDtypeStruct((2, SC, NCLS), jnp.float32),
        in_specs=[pl.BlockSpec(memory_space=pltpu.SMEM)] + [vmem] * 5 + [hbm] * 4,
        out_specs=vmem,
        scratch_shapes=[
            pltpu.VMEM((PV, D), bf),
            pltpu.VMEM((D, 3 * D), bf),
            pltpu.VMEM((D, D), bf),
            pltpu.VMEM((D, NCLS), bf),
            dma((4,)),
            pltpu.VMEM((N, MOST, 16, FH), bf),
            pltpu.VMEM((N, MOST, 16, FH), bf),
            pltpu.VMEM((N, 16, FH), bf),
            pltpu.VMEM((2, 8, 16, FH), bf),
            pltpu.VMEM((8, 16, D), bf),
            pltpu.VMEM((2, 128, D), bf),
            pltpu.VMEM((128, D), jnp.float32),
            pltpu.VMEM((128, D), bf),
            pltpu.VMEM((N, 2, 96, D), bf),
            pltpu.VMEM((N, 2, 32, D), bf),
            pltpu.VMEM((N, 192, 128), bf),
            pltpu.VMEM((N, 192, 128), bf),
            pltpu.VMEM((64, 2048), bf),
            pltpu.VMEM((2048, 64), bf),
            pltpu.VMEM((64, 2048), bf),
            pltpu.VMEM((N, 64, 128), bf),
            pltpu.VMEM((N, 64, 128), bf),
            pltpu.VMEM((8, 16, NCLS), bf),
            pltpu.VMEM((8, 16, NCLS), bf),
            pltpu.VMEM((N, MOST, 16, NCLS), bf),
            pltpu.VMEM((N, MOST, 16, NCLS), bf),
            pltpu.SemaphoreType.REGULAR,
            dma((N,)), dma((N,)), dma((N,)), dma((N,)), dma((N,)), dma((8,)), dma, dma,
            dma((3,)), dma((12,)), dma((N,)), dma((N,)), dma((N,)),
            dma((3,)), dma((12,)), dma((N,)), dma((N,)), dma((N,)),
            dma((N,)), dma((N,)), dma((N,)), dma((N,)), dma((8,)), dma((8,)), dma((N,)), dma((N,)),
        ],
        compiler_params=pltpu.CompilerParams(
            collective_id=0, has_side_effects=True, vmem_limit_bytes=56 * 1024 * 1024
        ),
    )(
        tile_list, scene_band, pos, wq, wo, norm_gains,
        embed_weight, window_qkv, window_out, head_weight,
    )


def solution(mesh):
    return jax.shard_map(
        local,
        mesh=mesh,
        in_specs=(
            P("seq", "tile", None), P(), P(), P("seq", None), P(), P(), P(),
            P(None, "seq"), P("seq", None), P(),
        ),
        out_specs=P("seq", "tile", None),
        check_vma=False,
    )
```

time: 686 us -> 125 us (0.18); the launches traced: 674 us -> 125 us
  waiting for transfers between devices: 231 us -> 0 us
  local copies, waits for them, and re-layouts: 228 us -> 4.47 us
  starting transfers between devices: 146 us -> 0 us
  Pallas kernels: 0 us -> 120 us
  matrix products: 27.5 us -> 0 us
  between operations: 22 us -> 0.01 us
  other arithmetic: 18.5 us -> 0 us
    concatenate x32 -> x0, local copies, waits for them, and re-layouts: 145 us -> none  [the longest x31 145 us: local(): jnp.concatenate([by_window(piece, band_rows, tile_cols) for piece in pair...]
    ppermute x14 -> x0, starting transfers between devices: 125 us -> none  [passed_along(): return lax.ppermute(array, axis, pairs)]
    pallas_call x0 -> x1, Pallas kernels: none -> 120 us  [local(): pl.pallas_call(kernel, out_shape=jax.ShapeDtypeStruct((2, SC, NCLS), jnp....]
    reduce_scatter x1 -> x0, waiting for transfers between devices: 87 us -> none  [local(): lax.psum_scatter(jnp.dot(attended, global_out, preferred_element_type=jnp...]
    all_gather x1 -> x0, waiting for transfers between devices: 85.4 us -> none  [local(): features = lax.all_gather(normed, 'seq', axis=0, tiled=True)]
    ppermute x14 -> x0, waiting for transfers between devices: 34.6 us -> none  [passed_along(): return lax.ppermute(array, axis, pairs)]
    ppermute x14 -> x0, local copies, waits for them, and re-layouts: 28.5 us -> none  [passed_along(): return lax.ppermute(array, axis, pairs)]
    transpose x18 -> x0, local copies, waits for them, and re-layouts: 28.2 us -> none  [the longest x16 28.1 us: by_window(): matrix.reshape(band_rows, tile_cols // WIN, WIN, width)]
  transfers between devices with their start and end apart: 20 -> 0, of which waited for: 8 -> 0; matrix products, arithmetic and copies ran while one was open for 26% -> 0% of each run, Pallas kernels for 0% -> 0%
where the time goes in v1:
time: 125 us
  Pallas kernels  120 us (96%)
  local copies, waits for them, and re-layouts  4.47 us (4%)
    pallas_call x1, Pallas kernels, local(): pl.pallas_call(kernel, out_shape=jax.ShapeDtypeStruct((2, SC, NCLS), jnp....  120 us
    unnamed x4, local copies, waits for them, and re-layouts  3.85 us

profile of v1, /device:TPU:1, one launch (start us, length us, event | category | flops | bytes accessed | tf_op | source)
XLA Modules:
  0.0 124.7 jit_solution(14012613278788228816)
XLA Ops:
  0.0 0.0 copy-start
  0.0 0.9 copy-done
  1.0 1.4 %copy.11.tl = s32[16,3]{1,0:T(8,128)} copy(s32[16,3]{0,1:T(4,128)} %param.11) | data formatting | bytes 384 | tf_op args[1]
  2.3 0.6 dynamic-slice_bitcast_fusion.pos
  2.9 120.2 %shard_map.100 = f32[2,96,128]{2,1,0:T(8,128)} custom-call(s32[16,3]{1,0:T(8,128)} %copy.11.tl, bf16[2,96,768]{2,1,0:T(8,128)(2,1)} %strip.1, bf16[16,1024]{1,0:T(8,128)(2,1)} %dynamic-slice_bitcast_fusion.pos, bf16[2,96,1024]{2,1,0:T(8,128)(2,1)} %bitcast.8, bf16[2,32,1024]{2,1,0:T(8,128)(2,1)} %bitcast.9, f32[3,1024]{1,0:T(4,128)} %gains.1, ...), custom_call_target="tpu_custom_call" | custom-call | tf_op jit(solution)/shard_map/pallas_call | solution.py:473
  123.1 1.5 %copy.13 = f32[2,96,128]{2,1,0:T(8,128)} copy(f32[2,96,128]{2,1,0:T(8,128)} %shard_map.100) | data formatting | bytes 196608
Async XLA Ops:
  0.0 1.0 copy-start

commit v2 on v1

--- a/solution.py
+++ b/solution.py
@@ -46,8 +46,8 @@
 
 
 def kernel(
-    tl, strip, pos, wq, wo, gains, we_hbm, w1_hbm, wout_hbm, hw_hbm, out_ref,
-    we, w1, wout, hw, load_sem,
+    tl_hbm, strip, pos, wq, wo, gains, we_hbm, w1_hbm, wout_hbm, hw_hbm, out_ref,
+    tl, we, w1, wout, hw, load_sem,
     out1, in1, fwd, pix, posall, nbuf, x_ref, o1,
     wqall, woall, q_out, q_in, qt, kb, vt, o_out, o_in,
     lout, lin, rout, rin,
@@ -73,6 +73,7 @@
         pltpu.make_async_copy(w1_hbm, w1, load_sem.at[1]),
         pltpu.make_async_copy(wout_hbm, wout, load_sem.at[2]),
         pltpu.make_async_copy(hw_hbm, hw, load_sem.at[3]),
+        pltpu.make_async_copy(tl_hbm, tl, load_sem.at[4]),
     ]
     for load in loads:
         load.start()
@@ -89,6 +90,7 @@
 
     loop(1, N, greet)
 
+    loads[4].wait()
     owners = [tl[t, 0] for t in range(N)]
     starts = [tl[t, 1] - tl[t, 2] for t in range(N)]
     ranks = []
@@ -136,75 +138,121 @@
 
     loop(1, N, greet_again)
 
-    def pos_copy(t):
-        return remote(pos, posall.at[rm], pos_s.at[t], pos_r.at[rm], i, t)
+    def pos_z(k):
+        return remote(
+            pos, posall.at[rm], pos_s.at[k - 1], pos_r.at[rm], i, x_at * 4 + (z_at + k) % 4
+        )
+
+    block = x_at % 2
+
+    def pos_x(k):
+        half = posall.at[pl.ds(4 * block, 4)]
+        return remote(
+            half, half, pos_s.at[k + 2], pos_r.at[8 + block], i, ((x_at + k) % 4) * 4 + z_at
+        )
+
+    def place(dx, dz):
+        return ((x_at + dx) % 4) * 4 + (z_at + dz) % 4
+
+    def piece(full, shard, part):
+        rows = full.shape[2]
+        if part == 2:
+            return full.at[shard, core]
+        return full.at[shard, core, pl.ds(part * (rows // 2), rows // 2)]
+
+    def along(full, sems, got, step, axis, part, shard, number):
+        if axis == 0:
+            to = x_at * 4 + (z_at + step) % 4
+        else:
+            to = ((x_at + step) % 4) * 4 + z_at
+        at = piece(full, shard, part)
+        return remote(at, at, sems.at[number], got.at[part, shard], i, to)
+
+    def arrived(full, sems, got, part, shard):
+        at = piece(full, shard, part)
+        remote(at, at, sems.at[0], got.at[part, shard], i, r).wait_recv()
+
+    def to_sibling(full, ss, sgot, shard):
+        at = full.at[shard, core]
+        return remote(at, at, ss.at[shard], sgot.at[shard], sibling, r)
+
+    def from_sibling(full, ss, sgot, shard):
+        at = full.at[shard, 1 - core]
+        return remote(at, at, ss.at[shard], sgot.at[shard], sibling, r)
+
+    def gather_copies(full, zs, xs, got):
+        result = {}
+        for n, step in enumerate((1, 3)):
+            result["z", step] = along(full, zs, got, step, 0, 2, place(0, 0), n)
+            result["zz", step] = along(full, zs, got, step, 0, n, place(0, 4 - step), 2 + n)
+            for dz in range(4):
+                result["x", dz, step] = along(
+                    full, xs, got, step, 1, 2, place(0, dz), dz * 4 + n
+                )
+                result["xx", dz, step] = along(
+                    full, xs, got, step, 1, n, place(4 - step, dz), dz * 4 + 2 + n
+                )
+        return result
+
+    def gather_steps(src, full, zs, xs, ss, got, sgot):
+        copies = gather_copies(full, zs, xs, got)
+
+        def own():
+            full[r] = src[...]
+            for step in (1, 3):
+                copies["z", step].start()
+            for step in (1, 3):
+                copies["x", 0, step].start()
+
+        def pass_z():
+            for step in (1, 3):
+                dz = 4 - step
+                arrived(full, zs, got, 2, place(0, dz))
+                copies["zz", step].start()
+                copies["x", dz, 1].start()
+                copies["x", dz, 3].start()
+                to_sibling(full, ss, sgot, place(0, dz)).start()
+
+        def pass_zz():
+            for part in range(2):
+                arrived(full, zs, got, part, place(0, 2))
+            copies["x", 2, 1].start()
+            copies["x", 2, 3].start()
+            to_sibling(full, ss, sgot, place(0, 2)).start()
+
+        def pass_x(dz):
+            for step in (1, 3):
+                dx = 4 - step
+                arrived(full, zs, got, 2, place(dx, dz))
+                copies["xx", dz, step].start()
+                to_sibling(full, ss, sgot, place(dx, dz)).start()
+
+        def pass_xx(dz):
+            for part in range(2):
+                arrived(full, zs, got, part, place(2, dz))
+            to_sibling(full, ss, sgot, place(2, dz)).start()
+
+        def last():
+            loop(1, N, lambda k: from_sibling(full, ss, sgot, (r + k) % N).wait_recv())
+
+        def sent():
+            for copy in copies.values():
+                copy.wait_send()
+            loop(1, N, lambda k: to_sibling(full, ss, sgot, (r + k) % N).wait_send())
+
+        return own, pass_z, pass_zz, pass_x, pass_xx, last, sent
+
+    qg = gather_steps(wq, wqall, qzs, qxs, qss, qr, qsr)
+    og = gather_steps(wo, woall, ozs, oxs, oss, orr, osr)
+
+    qg[0]()
 
     @pl.when(upper == r8)
     def _():
-        loop(1, N, lambda k: pos_copy((r + k) % N).start())
         posall[rm] = pos[...]
-
-    def along_z(src, full, zs, got, k):
-        return remote(
-            src.at[core], full.at[r, core], zs.at[k - 1], got.at[r], i, x_at * 4 + (z_at + k) % 4
-        )
-
-    def along_x(src, full, xs, got, z, k):
-        shard = x_at * 4 + z
-        piece = src.at[core] if src is not None else full.at[shard, core]
-        return remote(
-            piece, full.at[shard, core], xs.at[z * 3 + k - 1], got.at[shard],
-            i, ((x_at + k) % 4) * 4 + z_at,
-        )
-
-    def arrival(src, full, zs, got, shard):
-        return remote(src.at[core], full.at[shard, core], zs.at[0], got.at[shard], i, r)
-
-    def to_sibling(full, ss, got, shard):
-        return remote(
-            full.at[shard, core], full.at[shard, core], ss.at[shard], got.at[shard], sibling, r
-        )
-
-    def from_sibling(full, ss, got, shard):
-        return remote(
-            full.at[shard, 1 - core], full.at[shard, 1 - core], ss.at[shard], got.at[shard],
-            sibling, r,
-        )
-
-    def spread_own(src, full, zs, xs, got):
         for k in range(1, 4):
-            along_z(src, full, zs, got, k).start()
-        for k in range(1, 4):
-            along_x(src, full, xs, got, z_at, k).start()
-        full[r] = src[...]
-
-    def pass_z(src, full, zs, xs, ss, got, sgot):
-        def one(k):
-            z = (z_at + k) % 4
-            arrival(src, full, zs, got, x_at * 4 + z).wait_recv()
-            for d in range(1, 4):
-                along_x(None, full, xs, got, z, d).start()
-            to_sibling(full, ss, sgot, x_at * 4 + z).start()
-
-        loop(1, 4, one)
-
-    def pass_x(src, full, zs, ss, got, sgot, k):
-        z = (z_at + k) % 4
-        for d in range(1, 4):
-            shard = ((x_at + d) % 4) * 4 + z
-            arrival(src, full, zs, got, shard).wait_recv()
-            to_sibling(full, ss, sgot, shard).start()
-
-    def finish_sends(src, full, zs, xs, ss, got, sgot):
-        for k in range(1, 4):
-            along_z(src, full, zs, got, k).wait_send()
-        for k in range(0, 4):
-            for d in range(1, 4):
-                along_x(None, full, xs, got, (z_at + k) % 4, d).wait_send()
-
-        loop(1, N, lambda k: to_sibling(full, ss, sgot, (r + k) % N).wait_send())
-
-    spread_own(wq, wqall, qzs, qxs, qr)
+            pos_z(k).start()
+
 
     loop(1, N, lambda k: p1_in((i + k) % N).wait_recv())
     for t in range(N):
@@ -229,7 +277,16 @@
     def _():
         pix[core, rm] = fwd[r]
 
-    pass_z(wq, wqall, qzs, qxs, qss, qr, qsr)
+    @pl.when(upper == r8)
+    def _():
+        for k in range(1, 4):
+            other = 4 * block + (z_at + k) % 4
+            remote(pos, posall.at[other], pos_s.at[0], pos_r.at[other], i, r).wait_recv()
+        for k in range(1, 4):
+            pos_x(k).start()
+
+    qg[1]()
+    qg[3](0)
 
     for f in range(2):
         source = band * 4 + core * 2 + f
@@ -243,12 +300,13 @@
 
         loop(0, 8, p2_in)
 
-    def pos_in(k):
-        @pl.when(upper * 8 + k != r)
-        def _():
-            remote(pos, posall.at[k], pos_s.at[0], pos_r.at[k], i, r).wait_recv()
-
-    loop(0, 8, pos_in)
+    for e in range(2):
+
+        @pl.when(2 * upper + e != x_at)
+        def _(e=e):
+            half = posall.at[pl.ds(4 * e, 4)]
+            remote(half, half, pos_s.at[0], pos_r.at[8 + e], i, r).wait_recv()
+
     loads[0].wait()
     stream = dot(pix[0].reshape(128, FH), we[0:FH]) + dot(pix[1].reshape(128, FH), we[FH:PV])
     stream = stream + posall[...].reshape(128, D).astype(jnp.float32)
@@ -257,6 +315,8 @@
     sib = remote(nbuf.at[core], nbuf.at[core], sib_s, sib_r, sibling, r)
     sib.start()
     sib_in = remote(nbuf.at[1 - core], nbuf.at[1 - core], sib_s, sib_r, sibling, r)
+    qg[2]()
+    qg[4](0)
     loads[1].wait()
     sib_in.wait_recv()
 
@@ -280,33 +340,53 @@
             results, axis=1
         ).astype(jnp.bfloat16)
 
-    loop(0, 4, window_heads)
-    pass_x(wq, wqall, qzs, qss, qr, qsr, 0)
+    loop(0, 2, window_heads)
+    qg[3](1)
+    loop(2, 4, window_heads)
+    qg[3](3)
+    qg[4](1)
     loop(4, 8, window_heads)
     loads[2].wait()
     stream = x_ref[...] + dot(o1[...], wout[...])
     x_ref[...] = stream
     normed = layer_norm(stream, gains[1:2])
-    for k in range(1, 4):
-        pass_x(wq, wqall, qzs, qss, qr, qsr, k)
-    loop(1, N, lambda k: from_sibling(wqall, qss, qsr, (r + k) % N).wait_recv())
-
-    def to_head(h):
-        return remote(q_out.at[h], q_in.at[i], as_.at[h], ar.at[i], h, r)
-
-    def project(k):
-        h = (i + k) % N
-        q_out[h] = lax.dot_general(
-            wqall[h].reshape(192, D), normed, NT, preferred_element_type=jnp.float32
-        ).astype(jnp.bfloat16)
-        to_head(h).start()
-
-    loop(1, N, project)
-    q_in[i] = lax.dot_general(
-        wqall[i].reshape(192, D), normed, NT, preferred_element_type=jnp.float32
-    ).astype(jnp.bfloat16)
-
-    spread_own(wo, woall, ozs, oxs, orr)
+    my_head = band * 4 + (i % 4 + 4 - band) % 4
+
+    def to_head(x, z):
+        h = x * 4 + z
+        return remote(q_out.at[h], q_in.at[i], as_.at[h], ar.at[i], x * 4 + (z + x) % 4, r)
+
+    def project(dz):
+        for dx in range(4):
+            if dx > 0 or dz > 0:
+                from_sibling(wqall, qss, qsr, place(dx, dz)).wait_recv()
+        z = (z_at + dz) % 4
+        for k in range(4):
+            x = (band + k) % 4
+            h = x * 4 + z
+            q_out[h] = lax.dot_general(
+                wqall[h].reshape(192, D), normed, NT, preferred_element_type=jnp.float32
+            ).astype(jnp.bfloat16)
+            if k > 0:
+                to_head(x, z).start()
+            else:
+
+                @pl.when(h != my_head)
+                def _(x=x, z=z):
+                    to_head(x, z).start()
+
+                @pl.when(h == my_head)
+                def _(h=h):
+                    q_in[i] = q_out[h]
+
+    qg[3](2)
+    project(0)
+    project(1)
+    qg[4](3)
+    project(3)
+    og[0]()
+    qg[4](2)
+    project(2)
 
     def head_in(k):
         s = (i + k) % N
@@ -320,7 +400,7 @@
         vt[:, at : at + 128] = q_in[s, 128:192]
 
     def home(j):
-        return remote(o_out.at[j], o_in.at[i], bs.at[j], br.at[i], j, r)
+        return remote(o_out.at[j], o_in.at[my_head], bs.at[j], br.at[my_head], j, r)
 
     def attend(k):
         b = (k + i // 2 + 1) % 8
@@ -339,18 +419,26 @@
             def _(j=j):
                 home(j).start()
 
+    og[1]()
+    og[3](0)
     loop(0, 2, attend)
-    pass_z(wo, woall, ozs, oxs, oss, orr, osr)
-    loop(2, 7, attend)
-    for k in range(0, 4):
-        pass_x(wo, woall, ozs, oss, orr, osr, k)
-    loop(7, 8, attend)
-    o_in[i] = o_out[i]
-    loop(1, N, lambda k: from_sibling(woall, oss, osr, (r + k) % N).wait_recv())
+    og[2]()
+    og[4](0)
+    og[3](1)
+    loop(2, 4, attend)
+    og[3](3)
+    og[4](1)
+    loop(4, 6, attend)
+    og[3](2)
+    og[4](3)
+    loop(6, 8, attend)
+    og[4](2)
+    o_in[my_head] = o_out[i]
+    og[5]()
 
     def home_in(k):
-        s = (i + k) % N
-        remote(o_out.at[s], o_in.at[s], bs.at[s], br.at[s], s, r).wait_recv()
+        s = (my_head + k) % N
+        remote(o_out.at[s], o_in.at[s], bs.at[s], br.at[s], i, r).wait_recv()
 
     loop(1, N, home_in)
     attended = o_in[...].reshape(D, 128).astype(jnp.float32).T.astype(jnp.bfloat16)
@@ -434,7 +522,9 @@
 
     @pl.when(upper == r8)
     def _():
-        loop(1, N, lambda k: pos_copy((r + k) % N).wait_send())
+        for k in range(1, 4):
+            pos_z(k).wait_send()
+            pos_x(k).wait_send()
 
     loop(1, N, lambda k: p2((r + k) % N).wait_send())
 
@@ -443,9 +533,12 @@
         p2(r).wait_send()
 
     sib.wait_send()
-    finish_sends(wq, wqall, qzs, qxs, qss, qr, qsr)
-    finish_sends(wo, woall, ozs, oxs, oss, orr, osr)
-    loop(1, N, lambda k: to_head((i + k) % N).wait_send())
+    qg[6]()
+    og[6]()
+    loop(
+        1, N,
+        lambda k: to_head(((my_head + k) % N) // 4, (my_head + k) % 4).wait_send(),
+    )
     loop(1, N, lambda k: home((i + k) % N).wait_send())
 
     def l1_sent(k):
@@ -473,14 +566,15 @@
     return pl.pallas_call(
         kernel,
         out_shape=jax.ShapeDtypeStruct((2, SC, NCLS), jnp.float32),
-        in_specs=[pl.BlockSpec(memory_space=pltpu.SMEM)] + [vmem] * 5 + [hbm] * 4,
+        in_specs=[hbm] + [vmem] * 5 + [hbm] * 4,
         out_specs=vmem,
         scratch_shapes=[
+            pltpu.SMEM((N, 3), jnp.int32),
             pltpu.VMEM((PV, D), bf),
             pltpu.VMEM((D, 3 * D), bf),
             pltpu.VMEM((D, D), bf),
             pltpu.VMEM((D, NCLS), bf),
-            dma((4,)),
+            dma((5,)),
             pltpu.VMEM((N, MOST, 16, FH), bf),
             pltpu.VMEM((N, MOST, 16, FH), bf),
             pltpu.VMEM((N, 16, FH), bf),
@@ -503,9 +597,9 @@
             pltpu.VMEM((N, MOST, 16, NCLS), bf),
             pltpu.VMEM((N, MOST, 16, NCLS), bf),
             pltpu.SemaphoreType.REGULAR,
-            dma((N,)), dma((N,)), dma((N,)), dma((N,)), dma((N,)), dma((8,)), dma, dma,
-            dma((3,)), dma((12,)), dma((N,)), dma((N,)), dma((N,)),
-            dma((3,)), dma((12,)), dma((N,)), dma((N,)), dma((N,)),
+            dma((N,)), dma((N,)), dma((N,)), dma((N,)), dma((6,)), dma((10,)), dma, dma,
+            dma((4,)), dma((N,)), dma((N,)), dma((3, N)), dma((N,)),
+            dma((4,)), dma((N,)), dma((N,)), dma((3, N)), dma((N,)),
             dma((N,)), dma((N,)), dma((N,)), dma((N,)), dma((8,)), dma((8,)), dma((N,)), dma((N,)),
         ],
         compiler_params=pltpu.CompilerParams(

time: 125 us -> 117 us (0.936)
  Pallas kernels: 120 us -> 112 us
    pallas_call x1, Pallas kernels: 120 us -> 112 us  [local(): pl.pallas_call(kernel, out_shape=jax.ShapeDtypeStruct((2, SC, NCLS), jnp....]
where the time goes in v2:
time: 117 us
  Pallas kernels  112 us (96%)
  local copies, waits for them, and re-layouts  4.47 us (4%)
    pallas_call x1, Pallas kernels, local(): pl.pallas_call(kernel, out_shape=jax.ShapeDtypeStruct((2, SC, NCLS), jnp....  112 us
    unnamed x4, local copies, waits for them, and re-layouts  3.85 us

profile of v2, /device:TPU:1, one launch (start us, length us, event | category | flops | bytes accessed | tf_op | source)
XLA Modules:
  0.0 116.9 jit_solution(2464761776534409779)
XLA Ops:
  0.0 0.0 copy-start
  0.0 0.9 copy-done
  1.0 1.4 %copy.11.tl_hbm = s32[16,3]{1,0:T(8,128)} copy(s32[16,3]{0,1:T(4,128)} %param.11) | data formatting | bytes 384 | tf_op args[1]
  2.3 0.6 dynamic-slice_bitcast_fusion.pos
  2.9 112.4 %shard_map.100 = f32[2,96,128]{2,1,0:T(8,128)} custom-call(s32[16,3]{1,0:T(8,128)} %copy.11.tl_hbm, bf16[2,96,768]{2,1,0:T(8,128)(2,1)} %strip.1, bf16[16,1024]{1,0:T(8,128)(2,1)} %dynamic-slice_bitcast_fusion.pos, bf16[2,96,1024]{2,1,0:T(8,128)(2,1)} %bitcast.8, bf16[2,32,1024]{2,1,0:T(8,128)(2,1)} %bitcast.9, f32[3,1024]{1,0:T(4,128)} %gains.1, ...), custom_call_target="tpu_custom_call" | custom-call | tf_op jit(solution)/shard_map/pallas_call | solution.py:566
  115.3 1.5 %copy.13 = f32[2,96,128]{2,1,0:T(8,128)} copy(f32[2,96,128]{2,1,0:T(8,128)} %shard_map.100) | data formatting | bytes 196608
Async XLA Ops:
  0.0 1.0 copy-start

commit v3 on v2

--- a/solution.py
+++ b/solution.py
@@ -51,9 +51,9 @@
     out1, in1, fwd, pix, posall, nbuf, x_ref, o1,
     wqall, woall, q_out, q_in, qt, kb, vt, o_out, o_in,
     lout, lin, rout, rin,
-    entered,
+    nall, entered, ns, nr,
     p1s, p1r, p2s, p2r, pos_s, pos_r, sib_s, sib_r,
-    qzs, qxs, qss, qr, qsr, ozs, oxs, oss, orr, osr,
+    qzs, qss, qr, qsr, ozs, oxs, oss, orr, osr,
     as_, ar, bs, br, l1s, l1r, l2s, l2r,
 ):
     i = lax.axis_index("tile")
@@ -62,11 +62,22 @@
     sibling = i + 1 - 2 * core
     x_at = r // 4
     z_at = r % 4
-    band = i // 4
-    upper = (i % 4) // 2
-    kc_mine = 2 * band + core
+    y_at = i // 4
+    z_low = (i % 4) // 2
+    y_high = y_at // 2
+    upper = y_at % 2
+    kc_mine = 2 * x_at + core
+    my_tile = z_at * 4 + z_low * 2 + y_high
+    fourth = upper * 2 + core
+    my_head = x_at * 4 + fourth
     r8 = r // 8
     rm = r % 8
+
+    def worker(t, a, b, half):
+        return ((t % 2) * 2 + a) * 4 + ((t // 2) % 2) * 2 + half, b * 4 + t // 4
+
+    def member(quarter):
+        return (y_high * 2 + quarter // 2) * 4 + z_low * 2 + quarter % 2
 
     loads = [
         pltpu.make_async_copy(we_hbm, we, load_sem.at[0]),
@@ -138,18 +149,31 @@
 
     loop(1, N, greet_again)
 
-    def pos_z(k):
+    aside = jnp.where(upper == r8, 0, 1)
+
+    def pos_copy(n):
+        to = 2 * (n // 4) + aside
         return remote(
-            pos, posall.at[rm], pos_s.at[k - 1], pos_r.at[rm], i, x_at * 4 + (z_at + k) % 4
-        )
-
-    block = x_at % 2
-
-    def pos_x(k):
-        half = posall.at[pl.ds(4 * block, 4)]
-        return remote(
-            half, half, pos_s.at[k + 2], pos_r.at[8 + block], i, ((x_at + k) % 4) * 4 + z_at
-        )
+            pos.at[to], posall.at[rm], pos_s.at[n], pos_r.at[rm],
+            i + aside * (4 - 8 * upper), to * 4 + n % 4,
+        )
+
+    def pos_stays(n):
+        return (aside == 0) & ((2 * (n // 4)) * 4 + n % 4 == r)
+
+    def pos_start(n):
+        @pl.when(jnp.logical_not(pos_stays(n)))
+        def _():
+            pos_copy(n).start()
+
+        @pl.when(pos_stays(n))
+        def _():
+            posall[rm] = pos[x_at]
+
+    def pos_sent(n):
+        @pl.when(jnp.logical_not(pos_stays(n)))
+        def _():
+            pos_copy(n).wait_send()
 
     def place(dx, dz):
         return ((x_at + dx) % 4) * 4 + (z_at + dz) % 4
@@ -242,54 +266,74 @@
 
         return own, pass_z, pass_zz, pass_x, pass_xx, last, sent
 
-    qg = gather_steps(wq, wqall, qzs, qxs, qss, qr, qsr)
+    def weights_at(z, part):
+        if part == 2:
+            return wqall.at[z % 4, core]
+        return wqall.at[z % 4, core, pl.ds(part * 48, 48)]
+
+    def weights_z(step, part, z, number):
+        at = weights_at(z, part)
+        return remote(
+            at, at, qzs.at[number], qr.at[part, z % 4], i, x_at * 4 + (z_at + step) % 4
+        )
+
+    weights_copies = [
+        weights_z(1, 2, z_at, 0),
+        weights_z(3, 2, z_at, 1),
+        weights_z(1, 0, z_at + 3, 2),
+        weights_z(3, 1, z_at + 1, 3),
+    ]
+
+    def weights_in(z, part):
+        at = weights_at(z, part)
+        remote(at, at, qzs.at[0], qr.at[part, z % 4], i, r).wait_recv()
+
+    def weights_sibling(k):
+        z = (z_at + k) % 4
+        at = wqall.at[z, core]
+        return remote(at, at, qss.at[z], qsr.at[z], sibling, r)
+
+    def pass_weights():
+        weights_in(z_at + 3, 2)
+        weights_copies[2].start()
+        weights_sibling(3).start()
+        weights_in(z_at + 1, 2)
+        weights_copies[3].start()
+        weights_sibling(1).start()
+
+    def pass_weights_last():
+        weights_in(z_at + 2, 0)
+        weights_in(z_at + 2, 1)
+        weights_sibling(2).start()
+
     og = gather_steps(wo, woall, ozs, oxs, oss, orr, osr)
 
-    qg[0]()
-
-    @pl.when(upper == r8)
-    def _():
-        posall[rm] = pos[...]
-        for k in range(1, 4):
-            pos_z(k).start()
-
-
+    pl.semaphore_wait(entered, N - 1)
+    loop(0, 8, pos_start)
     loop(1, N, lambda k: p1_in((i + k) % N).wait_recv())
     for t in range(N):
         fwd[t] = in1[owners[t], ranks[t]]
-    pl.semaphore_wait(entered, N - 1)
-
-    half_c = (i % 4) // 2
-    worker = band * 4 + r8 * 2 + half_c
 
     def p2(t):
+        tile, seq = worker(t, r8, y_at, z_low)
         return remote(
-            fwd.at[t], pix.at[core, rm], p2s.at[t], p2r.at[core * 8 + rm], worker, t
-        )
-
-    loop(1, N, lambda k: p2((r + k) % N).start())
-
-    @pl.when(worker != i)
+            fwd.at[t], pix.at[core, rm], p2s.at[t], p2r.at[core * 8 + rm], tile, seq
+        )
+
+    home_tile, home_seq = worker(my_tile, r8, y_at, z_low)
+    away = (home_tile != i) | (home_seq != r)
+    loop(1, N, lambda k: p2((my_tile + k) % N).start())
+
+    @pl.when(away)
     def _():
-        p2(r).start()
-
-    @pl.when(worker == i)
+        p2(my_tile).start()
+
+    @pl.when(jnp.logical_not(away))
     def _():
-        pix[core, rm] = fwd[r]
-
-    @pl.when(upper == r8)
-    def _():
-        for k in range(1, 4):
-            other = 4 * block + (z_at + k) % 4
-            remote(pos, posall.at[other], pos_s.at[0], pos_r.at[other], i, r).wait_recv()
-        for k in range(1, 4):
-            pos_x(k).start()
-
-    qg[1]()
-    qg[3](0)
+        pix[core, rm] = fwd[my_tile]
 
     for f in range(2):
-        source = band * 4 + core * 2 + f
+        source = 2 * kc_mine + f
 
         def p2_in(k, f=f, source=source):
             @pl.when((source != i) | (upper * 8 + k != r))
@@ -300,13 +344,16 @@
 
         loop(0, 8, p2_in)
 
-    for e in range(2):
-
-        @pl.when(2 * upper + e != x_at)
-        def _(e=e):
-            half = posall.at[pl.ds(4 * e, 4)]
-            remote(half, half, pos_s.at[0], pos_r.at[8 + e], i, r).wait_recv()
-
+    def pos_in(k):
+        @pl.when((upper * 8 + k != r) | (x_at % 2 == 1))
+        def _():
+            remote(pos.at[0], posall.at[k], pos_s.at[0], pos_r.at[k], i, r).wait_recv()
+
+    loop(0, 8, pos_in)
+    wqall[z_at] = wq[...]
+    og[0]()
+    weights_copies[0].start()
+    weights_copies[1].start()
     loads[0].wait()
     stream = dot(pix[0].reshape(128, FH), we[0:FH]) + dot(pix[1].reshape(128, FH), we[FH:PV])
     stream = stream + posall[...].reshape(128, D).astype(jnp.float32)
@@ -315,8 +362,8 @@
     sib = remote(nbuf.at[core], nbuf.at[core], sib_s, sib_r, sibling, r)
     sib.start()
     sib_in = remote(nbuf.at[1 - core], nbuf.at[1 - core], sib_s, sib_r, sibling, r)
-    qg[2]()
-    qg[4](0)
+    og[1]()
+    og[3](0)
     loads[1].wait()
     sib_in.wait_recv()
 
@@ -341,58 +388,65 @@
         ).astype(jnp.bfloat16)
 
     loop(0, 2, window_heads)
-    qg[3](1)
+    og[2]()
+    pass_weights()
     loop(2, 4, window_heads)
-    qg[3](3)
-    qg[4](1)
-    loop(4, 8, window_heads)
+    og[4](0)
+    og[3](1)
+    loop(4, 6, window_heads)
+    og[3](3)
+    og[4](1)
+    loop(6, 8, window_heads)
+    og[3](2)
+    og[4](3)
+    pass_weights_last()
     loads[2].wait()
     stream = x_ref[...] + dot(o1[...], wout[...])
     x_ref[...] = stream
-    normed = layer_norm(stream, gains[1:2])
-    my_head = band * 4 + (i % 4 + 4 - band) % 4
-
-    def to_head(x, z):
-        h = x * 4 + z
-        return remote(q_out.at[h], q_in.at[i], as_.at[h], ar.at[i], x * 4 + (z + x) % 4, r)
-
-    def project(dz):
-        for dx in range(4):
-            if dx > 0 or dz > 0:
-                from_sibling(wqall, qss, qsr, place(dx, dz)).wait_recv()
-        z = (z_at + dz) % 4
-        for k in range(4):
-            x = (band + k) % 4
-            h = x * 4 + z
-            q_out[h] = lax.dot_general(
-                wqall[h].reshape(192, D), normed, NT, preferred_element_type=jnp.float32
+    nall[x_at] = layer_norm(stream, gains[1:2])
+
+    def tokens_x(k):
+        at = nall.at[x_at]
+        return remote(at, at, ns.at[k - 1], nr.at[x_at], i, ((x_at + k) % 4) * 4 + z_at)
+
+    for k in (1, 3, 2):
+        tokens_x(k).start()
+    for k in range(1, 4):
+        z = (z_at + k) % 4
+        at = wqall.at[z, 1 - core]
+        remote(at, at, qss.at[z], qsr.at[z], sibling, r).wait_recv()
+
+    def to_head(x, k):
+        quarter = (fourth + k) % 4
+        at = q_out.at[x * 4 + quarter]
+        return remote(
+            at, q_in.at[x * 4 + fourth], as_.at[x * 4 + quarter], ar.at[x * 4 + fourth],
+            member(quarter), r,
+        )
+
+    for step in (0, 1, 3, 2):
+        x = (x_at + step) % 4
+        if step > 0:
+            at = nall.at[x]
+            remote(at, at, ns.at[0], nr.at[x], i, r).wait_recv()
+        tokens = nall[x]
+        for k in (1, 2, 3, 0):
+            quarter = (fourth + k) % 4
+            found = lax.dot_general(
+                wqall[quarter].reshape(192, D), tokens, NT, preferred_element_type=jnp.float32
             ).astype(jnp.bfloat16)
             if k > 0:
-                to_head(x, z).start()
+                q_out[x * 4 + quarter] = found
+                to_head(x, k).start()
             else:
-
-                @pl.when(h != my_head)
-                def _(x=x, z=z):
-                    to_head(x, z).start()
-
-                @pl.when(h == my_head)
-                def _(h=h):
-                    q_in[i] = q_out[h]
-
-    qg[3](2)
-    project(0)
-    project(1)
-    qg[4](3)
-    project(3)
-    og[0]()
-    qg[4](2)
-    project(2)
-
-    def head_in(k):
-        s = (i + k) % N
-        remote(q_out.at[s], q_in.at[s], as_.at[s], ar.at[s], s, r).wait_recv()
-
-    loop(1, N, head_in)
+                q_in[x * 4 + fourth] = found
+
+    def head_in(x):
+        for k in range(1, 4):
+            s = x * 4 + (fourth + k) % 4
+            remote(q_out.at[s], q_in.at[s], as_.at[s], ar.at[s], i, r).wait_recv()
+
+    loop(0, 4, head_in)
     for s in range(N):
         at = s * 128
         qt[:, at : at + 128] = q_in[s, 0:64]
@@ -400,10 +454,13 @@
         vt[:, at : at + 128] = q_in[s, 128:192]
 
     def home(j):
-        return remote(o_out.at[j], o_in.at[my_head], bs.at[j], br.at[my_head], j, r)
+        return remote(
+            o_out.at[j], o_in.at[my_head], bs.at[j], br.at[my_head],
+            member(j % 4), (j // 4) * 4 + z_at,
+        )
 
     def attend(k):
-        b = (k + i // 2 + 1) % 8
+        b = (k + my_head // 2 + 1) % 8
         queries = qt[:, pl.ds(pl.multiple_of(b * 256, 256), 256)]
         scores = dot(kb[...], queries)
         top = jnp.max(scores, axis=0, keepdims=True)
@@ -415,25 +472,13 @@
         for e in range(2):
             j = 2 * b + e
 
-            @pl.when(j != i)
+            @pl.when(j != my_head)
             def _(j=j):
                 home(j).start()
 
-    og[1]()
-    og[3](0)
-    loop(0, 2, attend)
-    og[2]()
-    og[4](0)
-    og[3](1)
-    loop(2, 4, attend)
-    og[3](3)
-    og[4](1)
-    loop(4, 6, attend)
-    og[3](2)
-    og[4](3)
-    loop(6, 8, attend)
     og[4](2)
-    o_in[my_head] = o_out[i]
+    loop(0, 8, attend)
+    o_in[my_head] = o_out[my_head]
     og[5]()
 
     def home_in(k):
@@ -447,11 +492,11 @@
     logits = dot(layer_norm(stream, gains[2:3]), hw[...])
     lout[...] = logits.astype(jnp.bfloat16).reshape(8, 16, NCLS)
 
-    collector = 2 * kc_mine + r % 2
+    collector = 2 * kc_mine + my_tile % 2
 
     def l1(k):
         return remote(
-            lout.at[k], lin.at[r // 2], l1s.at[k], l1r.at[r // 2], collector, upper * 8 + k
+            lout.at[k], lin.at[my_tile // 2], l1s.at[k], l1r.at[my_tile // 2], collector, upper * 8 + k
         )
 
     def l1_start(k):
@@ -463,14 +508,15 @@
 
         @pl.when(jnp.logical_not(away))
         def _():
-            lin[r // 2] = lout[k]
+            lin[my_tile // 2] = lout[k]
 
     loop(0, 8, l1_start)
     kc = i // 2
-    giver = (kc // 2) * 4 + r8 * 2 + kc % 2
 
     def l1_in(k):
-        @pl.when((giver != i) | (2 * k + i % 2 != r))
+        giver, at = worker(2 * k + i % 2, r8, kc // 2, kc % 2)
+
+        @pl.when((giver != i) | (at != r))
         def _():
             remote(lout.at[0], lin.at[k], l1s.at[0], l1r.at[k], i, r).wait_recv()
 
@@ -520,26 +566,27 @@
 
     loop(1, N, lambda k: p1((i + k) % N).wait_send())
 
-    @pl.when(upper == r8)
+    loop(0, 8, pos_sent)
+    loop(1, N, lambda k: p2((my_tile + k) % N).wait_send())
+
+    @pl.when(away)
     def _():
+        p2(my_tile).wait_send()
+
+    sib.wait_send()
+    for k in range(1, 4):
+        weights_sibling(k).wait_send()
+        tokens_x(k).wait_send()
+    for copy in weights_copies:
+        copy.wait_send()
+    og[6]()
+
+    def heads_sent(x):
         for k in range(1, 4):
-            pos_z(k).wait_send()
-            pos_x(k).wait_send()
-
-    loop(1, N, lambda k: p2((r + k) % N).wait_send())
-
-    @pl.when(worker != i)
-    def _():
-        p2(r).wait_send()
-
-    sib.wait_send()
-    qg[6]()
-    og[6]()
-    loop(
-        1, N,
-        lambda k: to_head(((my_head + k) % N) // 4, (my_head + k) % 4).wait_send(),
-    )
-    loop(1, N, lambda k: home((i + k) % N).wait_send())
+            to_head(x, k).wait_send()
+
+    loop(0, 4, heads_sent)
+    loop(1, N, lambda k: home((my_head + k) % N).wait_send())
 
     def l1_sent(k):
         @pl.when((collector != i) | (upper * 8 + k != r))
@@ -554,9 +601,9 @@
     scene_band, tile_list, embed_weight, position, norm_gains, window_qkv, window_out,
     global_qkv, global_out, head_weight,
 ):
-    i = lax.axis_index("tile")
-    column = 2 * (i // 4) + i % 2
-    pos = lax.dynamic_slice_in_dim(position.reshape(2, 64, D), column * 8, 8, 1).reshape(16, D)
+    core = lax.axis_index("tile") % 2
+    parts = position.reshape(2, 4, 2, 8, D)
+    pos = lax.dynamic_index_in_dim(parts, core, 2, False).transpose(1, 0, 2, 3).reshape(4, 16, D)
     wq = global_qkv.T.reshape(2, 96, D)
     wo = global_out.reshape(2, 32, D)
     bf = jnp.bfloat16
@@ -583,7 +630,7 @@
             pltpu.VMEM((2, 128, D), bf),
             pltpu.VMEM((128, D), jnp.float32),
             pltpu.VMEM((128, D), bf),
-            pltpu.VMEM((N, 2, 96, D), bf),
+            pltpu.VMEM((4, 2, 96, D), bf),
             pltpu.VMEM((N, 2, 32, D), bf),
             pltpu.VMEM((N, 192, 128), bf),
             pltpu.VMEM((N, 192, 128), bf),
@@ -596,9 +643,11 @@
             pltpu.VMEM((8, 16, NCLS), bf),
             pltpu.VMEM((N, MOST, 16, NCLS), bf),
             pltpu.VMEM((N, MOST, 16, NCLS), bf),
+            pltpu.VMEM((4, 128, D), bf),
             pltpu.SemaphoreType.REGULAR,
-            dma((N,)), dma((N,)), dma((N,)), dma((N,)), dma((6,)), dma((10,)), dma, dma,
-            dma((4,)), dma((N,)), dma((N,)), dma((3, N)), dma((N,)),
+            dma((3,)), dma((4,)),
+            dma((N,)), dma((N,)), dma((N,)), dma((N,)), dma((8,)), dma((8,)), dma, dma,
+            dma((4,)), dma((4,)), dma((3, 4)), dma((4,)),
             dma((4,)), dma((N,)), dma((N,)), dma((3, N)), dma((N,)),
             dma((N,)), dma((N,)), dma((N,)), dma((N,)), dma((8,)), dma((8,)), dma((N,)), dma((N,)),
         ],

time: 117 us -> 112 us (0.957)
  Pallas kernels: 112 us -> 108 us
    pallas_call x1, Pallas kernels: 112 us -> 108 us  [local(): pl.pallas_call(kernel, out_shape=jax.ShapeDtypeStruct((2, SC, NCLS), jnp....]
where the time goes in v3:
time: 112 us
  Pallas kernels  108 us (96%)
  local copies, waits for them, and re-layouts  4.5 us (4%)
    pallas_call x1, Pallas kernels, local(): pl.pallas_call(kernel, out_shape=jax.ShapeDtypeStruct((2, SC, NCLS), jnp....  108 us
    unnamed x4, local copies, waits for them, and re-layouts  3.85 us

profile of v3, /device:TPU:1, one launch (start us, length us, event | category | flops | bytes accessed | tf_op | source)
XLA Modules:
  0.0 112.2 jit_solution(9162935994489272048)
XLA Ops:
  0.0 0.0 copy-start
  0.0 0.9 copy-done
  1.0 1.4 %copy.12.tl_hbm = s32[16,3]{1,0:T(8,128)} copy(s32[16,3]{0,1:T(4,128)} %param.11) | data formatting | bytes 384 | tf_op args[1]
  2.3 0.7 copy_bitcast_fusion.pos
  3.0 107.7 %shard_map.100 = f32[2,96,128]{2,1,0:T(8,128)} custom-call(s32[16,3]{1,0:T(8,128)} %copy.12.tl_hbm, bf16[2,96,768]{2,1,0:T(8,128)(2,1)} %strip.1, bf16[4,16,1024]{2,1,0:T(8,128)(2,1)} %copy_bitcast_fusion.pos, bf16[2,96,1024]{2,1,0:T(8,128)(2,1)} %bitcast.12, bf16[2,32,1024]{2,1,0:T(8,128)(2,1)} %bitcast.13, f32[3,1024]{1,0:T(4,128)} %gains.1, ...), custom_call_target="tpu_custom_call" | custom-call | tf_op jit(solution)/shard_map/pallas_call | solution.py:613
  110.7 1.5 %copy.15 = f32[2,96,128]{2,1,0:T(8,128)} copy(f32[2,96,128]{2,1,0:T(8,128)} %shard_map.100) | data formatting | bytes 196608
Async XLA Ops:
  0.0 1.0 copy-start

commit v4 on v3

--- a/solution.py
+++ b/solution.py
@@ -53,7 +53,7 @@
     lout, lin, rout, rin,
     nall, entered, ns, nr,
     p1s, p1r, p2s, p2r, pos_s, pos_r, sib_s, sib_r,
-    qzs, qss, qr, qsr, ozs, oxs, oss, orr, osr,
+    qzs, qss, qr, qsr, ozs, oxs, oss, obs, ozr, oxr, osr, obr,
     as_, ar, bs, br, l1s, l1r, l2s, l2r,
 ):
     i = lax.axis_index("tile")
@@ -178,94 +178,6 @@
     def place(dx, dz):
         return ((x_at + dx) % 4) * 4 + (z_at + dz) % 4
 
-    def piece(full, shard, part):
-        rows = full.shape[2]
-        if part == 2:
-            return full.at[shard, core]
-        return full.at[shard, core, pl.ds(part * (rows // 2), rows // 2)]
-
-    def along(full, sems, got, step, axis, part, shard, number):
-        if axis == 0:
-            to = x_at * 4 + (z_at + step) % 4
-        else:
-            to = ((x_at + step) % 4) * 4 + z_at
-        at = piece(full, shard, part)
-        return remote(at, at, sems.at[number], got.at[part, shard], i, to)
-
-    def arrived(full, sems, got, part, shard):
-        at = piece(full, shard, part)
-        remote(at, at, sems.at[0], got.at[part, shard], i, r).wait_recv()
-
-    def to_sibling(full, ss, sgot, shard):
-        at = full.at[shard, core]
-        return remote(at, at, ss.at[shard], sgot.at[shard], sibling, r)
-
-    def from_sibling(full, ss, sgot, shard):
-        at = full.at[shard, 1 - core]
-        return remote(at, at, ss.at[shard], sgot.at[shard], sibling, r)
-
-    def gather_copies(full, zs, xs, got):
-        result = {}
-        for n, step in enumerate((1, 3)):
-            result["z", step] = along(full, zs, got, step, 0, 2, place(0, 0), n)
-            result["zz", step] = along(full, zs, got, step, 0, n, place(0, 4 - step), 2 + n)
-            for dz in range(4):
-                result["x", dz, step] = along(
-                    full, xs, got, step, 1, 2, place(0, dz), dz * 4 + n
-                )
-                result["xx", dz, step] = along(
-                    full, xs, got, step, 1, n, place(4 - step, dz), dz * 4 + 2 + n
-                )
-        return result
-
-    def gather_steps(src, full, zs, xs, ss, got, sgot):
-        copies = gather_copies(full, zs, xs, got)
-
-        def own():
-            full[r] = src[...]
-            for step in (1, 3):
-                copies["z", step].start()
-            for step in (1, 3):
-                copies["x", 0, step].start()
-
-        def pass_z():
-            for step in (1, 3):
-                dz = 4 - step
-                arrived(full, zs, got, 2, place(0, dz))
-                copies["zz", step].start()
-                copies["x", dz, 1].start()
-                copies["x", dz, 3].start()
-                to_sibling(full, ss, sgot, place(0, dz)).start()
-
-        def pass_zz():
-            for part in range(2):
-                arrived(full, zs, got, part, place(0, 2))
-            copies["x", 2, 1].start()
-            copies["x", 2, 3].start()
-            to_sibling(full, ss, sgot, place(0, 2)).start()
-
-        def pass_x(dz):
-            for step in (1, 3):
-                dx = 4 - step
-                arrived(full, zs, got, 2, place(dx, dz))
-                copies["xx", dz, step].start()
-                to_sibling(full, ss, sgot, place(dx, dz)).start()
-
-        def pass_xx(dz):
-            for part in range(2):
-                arrived(full, zs, got, part, place(2, dz))
-            to_sibling(full, ss, sgot, place(2, dz)).start()
-
-        def last():
-            loop(1, N, lambda k: from_sibling(full, ss, sgot, (r + k) % N).wait_recv())
-
-        def sent():
-            for copy in copies.values():
-                copy.wait_send()
-            loop(1, N, lambda k: to_sibling(full, ss, sgot, (r + k) % N).wait_send())
-
-        return own, pass_z, pass_zz, pass_x, pass_xx, last, sent
-
     def weights_at(z, part):
         if part == 2:
             return wqall.at[z % 4, core]
@@ -306,7 +218,64 @@
         weights_in(z_at + 2, 1)
         weights_sibling(2).start()
 
-    og = gather_steps(wo, woall, ozs, oxs, oss, orr, osr)
+    def out_z(k):
+        return remote(
+            wo.at[core], woall.at[r, core], ozs.at[k - 1], ozr.at[z_at],
+            i, x_at * 4 + (z_at + k) % 4,
+        )
+
+    def out_z_sibling(k):
+        z = (z_at + k) % 4
+        at = woall.at[x_at * 4 + z, core]
+        return remote(at, at, oss.at[k - 1], osr.at[z], sibling, r)
+
+    def out_x(k):
+        at = woall.at[pl.ds(4 * x_at, 4), core]
+        return remote(at, at, oxs.at[k - 1], oxr.at[x_at], i, ((x_at + k) % 4) * 4 + z_at)
+
+    def out_x_sibling(k):
+        x = (x_at + k) % 4
+        at = woall.at[pl.ds(4 * x, 4), core]
+        return remote(at, at, obs.at[k - 1], obr.at[x], sibling, r)
+
+    def out_own():
+        woall[r] = wo[...]
+        for k in range(1, 4):
+            out_z(k).start()
+
+    def out_pass_z():
+        for k in range(1, 4):
+            z = (z_at + k) % 4
+            remote(
+                wo.at[core], woall.at[x_at * 4 + z, core], ozs.at[0], ozr.at[z], i, r
+            ).wait_recv()
+        for k in (1, 3, 2):
+            out_x(k).start()
+        for k in range(1, 4):
+            out_z_sibling(k).start()
+
+    def out_pass_x():
+        for k in (1, 3, 2):
+            x = (x_at + k) % 4
+            at = woall.at[pl.ds(4 * x, 4), core]
+            remote(at, at, oxs.at[0], oxr.at[x], i, r).wait_recv()
+            out_x_sibling(k).start()
+
+    def out_last():
+        for k in range(1, 4):
+            z = (z_at + k) % 4
+            at = woall.at[x_at * 4 + z, 1 - core]
+            remote(at, at, oss.at[0], osr.at[z], sibling, r).wait_recv()
+            x = (x_at + k) % 4
+            at = woall.at[pl.ds(4 * x, 4), 1 - core]
+            remote(at, at, obs.at[0], obr.at[x], sibling, r).wait_recv()
+
+    def out_sent():
+        for k in range(1, 4):
+            out_z(k).wait_send()
+            out_x(k).wait_send()
+            out_z_sibling(k).wait_send()
+            out_x_sibling(k).wait_send()
 
     pl.semaphore_wait(entered, N - 1)
     loop(0, 8, pos_start)
@@ -331,6 +300,8 @@
     @pl.when(jnp.logical_not(away))
     def _():
         pix[core, rm] = fwd[my_tile]
+
+    out_own()
 
     for f in range(2):
         source = 2 * kc_mine + f
@@ -351,7 +322,6 @@
 
     loop(0, 8, pos_in)
     wqall[z_at] = wq[...]
-    og[0]()
     weights_copies[0].start()
     weights_copies[1].start()
     loads[0].wait()
@@ -362,8 +332,7 @@
     sib = remote(nbuf.at[core], nbuf.at[core], sib_s, sib_r, sibling, r)
     sib.start()
     sib_in = remote(nbuf.at[1 - core], nbuf.at[1 - core], sib_s, sib_r, sibling, r)
-    og[1]()
-    og[3](0)
+    out_pass_z()
     loads[1].wait()
     sib_in.wait_recv()
 
@@ -387,19 +356,9 @@
             results, axis=1
         ).astype(jnp.bfloat16)
 
-    loop(0, 2, window_heads)
-    og[2]()
+    loop(0, 4, window_heads)
     pass_weights()
-    loop(2, 4, window_heads)
-    og[4](0)
-    og[3](1)
-    loop(4, 6, window_heads)
-    og[3](3)
-    og[4](1)
-    loop(6, 8, window_heads)
-    og[3](2)
-    og[4](3)
-    pass_weights_last()
+    loop(4, 8, window_heads)
     loads[2].wait()
     stream = x_ref[...] + dot(o1[...], wout[...])
     x_ref[...] = stream
@@ -411,6 +370,7 @@
 
     for k in (1, 3, 2):
         tokens_x(k).start()
+    pass_weights_last()
     for k in range(1, 4):
         z = (z_at + k) % 4
         at = wqall.at[z, 1 - core]
@@ -446,6 +406,7 @@
             s = x * 4 + (fourth + k) % 4
             remote(q_out.at[s], q_in.at[s], as_.at[s], ar.at[s], i, r).wait_recv()
 
+    out_pass_x()
     loop(0, 4, head_in)
     for s in range(N):
         at = s * 128
@@ -476,10 +437,9 @@
             def _(j=j):
                 home(j).start()
 
-    og[4](2)
     loop(0, 8, attend)
     o_in[my_head] = o_out[my_head]
-    og[5]()
+    out_last()
 
     def home_in(k):
         s = (my_head + k) % N
@@ -579,7 +539,7 @@
         tokens_x(k).wait_send()
     for copy in weights_copies:
         copy.wait_send()
-    og[6]()
+    out_sent()
 
     def heads_sent(x):
         for k in range(1, 4):
@@ -648,7 +608,7 @@
             dma((3,)), dma((4,)),
             dma((N,)), dma((N,)), dma((N,)), dma((N,)), dma((8,)), dma((8,)), dma, dma,
             dma((4,)), dma((4,)), dma((3, 4)), dma((4,)),
-            dma((4,)), dma((N,)), dma((N,)), dma((3, N)), dma((N,)),
+            dma((3,)), dma((3,)), dma((3,)), dma((3,)), dma((4,)), dma((4,)), dma((4,)), dma((4,)),
             dma((N,)), dma((N,)), dma((N,)), dma((N,)), dma((8,)), dma((8,)), dma((N,)), dma((N,)),
         ],
         compiler_params=pltpu.CompilerParams(

time: 112 us -> 105 us (0.938)
  Pallas kernels: 108 us -> 100 us
    pallas_call x1, Pallas kernels: 108 us -> 100 us  [local(): pl.pallas_call(kernel, out_shape=jax.ShapeDtypeStruct((2, SC, NCLS), jnp....]
where the time goes in v4:
time: 105 us
  Pallas kernels  100 us (95%)
  local copies, waits for them, and re-layouts  4.5 us (4%)
    pallas_call x1, Pallas kernels, local(): pl.pallas_call(kernel, out_shape=jax.ShapeDtypeStruct((2, SC, NCLS), jnp....  100 us
    unnamed x4, local copies, waits for them, and re-layouts  3.85 us

profile of v4, /device:TPU:1, one launch (start us, length us, event | category | flops | bytes accessed | tf_op | source)
XLA Modules:
  0.0 104.8 jit_solution(17543218140260311399)
XLA Ops:
  0.0 0.0 copy-start
  0.0 0.9 copy-done
  1.0 1.4 %copy.12.tl_hbm = s32[16,3]{1,0:T(8,128)} copy(s32[16,3]{0,1:T(4,128)} %param.11) | data formatting | bytes 384 | tf_op args[1]
  2.3 0.7 copy_bitcast_fusion.pos
  3.0 100.3 %shard_map.100 = f32[2,96,128]{2,1,0:T(8,128)} custom-call(s32[16,3]{1,0:T(8,128)} %copy.12.tl_hbm, bf16[2,96,768]{2,1,0:T(8,128)(2,1)} %strip.1, bf16[4,16,1024]{2,1,0:T(8,128)(2,1)} %copy_bitcast_fusion.pos, bf16[2,96,1024]{2,1,0:T(8,128)(2,1)} %bitcast.12, bf16[2,32,1024]{2,1,0:T(8,128)(2,1)} %bitcast.13, f32[3,1024]{1,0:T(4,128)} %gains.1, ...), custom_call_target="tpu_custom_call" | custom-call | tf_op jit(solution)/shard_map/pallas_call | solution.py:573
  103.3 1.5 %copy.15 = f32[2,96,128]{2,1,0:T(8,128)} copy(f32[2,96,128]{2,1,0:T(8,128)} %shard_map.100) | data formatting | bytes 196608
Async XLA Ops:
  0.0 1.0 copy-start

commit v5 on v4

--- a/solution.py
+++ b/solution.py
@@ -17,6 +17,7 @@
 NCLS = 128
 EPSILON = 1e-06
 FAR = 4096
+SCALE = HD ** (-0.5) * 1.4426950408889634
 NT = (((1,), (1,)), ((), ()))
 
 
@@ -336,29 +337,33 @@
     loads[1].wait()
     sib_in.wait_recv()
 
-    def window_heads(pair):
-        columns = w1[:, pl.ds(pl.multiple_of(pair * 384, 384), 384)]
-        mine = dot(nbuf[core], columns).astype(jnp.bfloat16)
-        other = dot(nbuf[1 - core], columns).astype(jnp.bfloat16)
-        both = jnp.concatenate([mine, other], axis=0)
+    def window_heads(quad):
+        columns = w1[:, pl.ds(pl.multiple_of(quad * 768, 768), 768)]
+        both = dot(nbuf[...].reshape(256, D), columns).astype(jnp.bfloat16)
+        scores = []
+        for h in range(4):
+            at = h * 192
+            mine = jnp.where(core == 0, both[:128, at : at + 64], both[128:, at : at + 64])
+            scores.append(
+                lax.dot_general(
+                    mine, both[:, at + 64 : at + 128], NT, preferred_element_type=jnp.float32
+                )
+            )
         results = []
-        for h in range(2):
+        for h in range(4):
             at = h * 192
-            scores = lax.dot_general(
-                mine[:, at : at + 64], both[:, at + 64 : at + 128], NT,
-                preferred_element_type=jnp.float32,
-            ) * HD ** (-0.5)
-            top = jnp.max(scores, axis=-1, keepdims=True)
-            weights = jnp.exp(scores - top)
-            weights = weights / jnp.sum(weights, axis=-1, keepdims=True)
-            results.append(dot(weights.astype(jnp.bfloat16), both[:, at + 128 : at + 192]))
-        o1[:, pl.ds(pl.multiple_of(pair * 128, 128), 128)] = jnp.concatenate(
+            top = jnp.max(scores[h], axis=-1, keepdims=True)
+            weights = jnp.exp2((scores[h] - top) * SCALE)
+            total = jnp.sum(weights, axis=-1, keepdims=True)
+            mixed = dot(weights.astype(jnp.bfloat16), both[:, at + 128 : at + 192])
+            results.append(mixed / total)
+        o1[:, pl.ds(pl.multiple_of(quad * 256, 256), 256)] = jnp.concatenate(
             results, axis=1
         ).astype(jnp.bfloat16)
 
-    loop(0, 4, window_heads)
+    loop(0, 2, window_heads)
     pass_weights()
-    loop(4, 8, window_heads)
+    loop(2, 4, window_heads)
     loads[2].wait()
     stream = x_ref[...] + dot(o1[...], wout[...])
     x_ref[...] = stream
@@ -421,23 +426,24 @@
         )
 
     def attend(k):
-        b = (k + my_head // 2 + 1) % 8
-        queries = qt[:, pl.ds(pl.multiple_of(b * 256, 256), 256)]
-        scores = dot(kb[...], queries)
-        top = jnp.max(scores, axis=0, keepdims=True)
-        weights = jnp.exp2((scores - top) * (HD ** (-0.5) * 1.4426950408889634))
-        total = jnp.sum(weights, axis=0, keepdims=True)
-        mixed = (dot(vt[...], weights.astype(jnp.bfloat16)) / total).astype(jnp.bfloat16)
-        o_out[2 * b] = mixed[:, 0:128]
-        o_out[2 * b + 1] = mixed[:, 128:256]
-        for e in range(2):
-            j = 2 * b + e
-
-            @pl.when(j != my_head)
-            def _(j=j):
-                home(j).start()
-
-    loop(0, 8, attend)
+        blocks = [(2 * k + e + my_head // 2 + 1) % 8 for e in range(2)]
+        scores = [
+            dot(kb[...], qt[:, pl.ds(pl.multiple_of(b * 256, 256), 256)]) for b in blocks
+        ]
+        for b, score in zip(blocks, scores):
+            top = jnp.max(score, axis=0, keepdims=True)
+            weights = jnp.exp2((score - top) * SCALE)
+            total = jnp.sum(weights, axis=0, keepdims=True)
+            mixed = (dot(vt[...], weights.astype(jnp.bfloat16)) / total).astype(jnp.bfloat16)
+            for e in range(2):
+                j = 2 * b + e
+                o_out[j] = mixed[:, 128 * e : 128 * e + 128]
+
+                @pl.when(j != my_head)
+                def _(j=j):
+                    home(j).start()
+
+    loop(0, 4, attend)
     o_in[my_head] = o_out[my_head]
     out_last()
 

time: 105 us -> 102 us (0.971)
  Pallas kernels: 100 us -> 97.2 us
    pallas_call x1, Pallas kernels: 100 us -> 97.2 us  [local(): pl.pallas_call(kernel, out_shape=jax.ShapeDtypeStruct((2, SC, NCLS), jnp....]
where the time goes in v5:
time: 102 us
  Pallas kernels  97.2 us (95%)
  local copies, waits for them, and re-layouts  4.5 us (4%)
    pallas_call x1, Pallas kernels, local(): pl.pallas_call(kernel, out_shape=jax.ShapeDtypeStruct((2, SC, NCLS), jnp....  97.2 us
    unnamed x4, local copies, waits for them, and re-layouts  3.85 us

profile of v5, /device:TPU:1, one launch (start us, length us, event | category | flops | bytes accessed | tf_op | source)
XLA Modules:
  0.0 101.7 jit_solution(11561447906701336739)
XLA Ops:
  0.0 0.0 copy-start
  0.0 0.9 copy-done
  1.0 1.4 %copy.12.tl_hbm = s32[16,3]{1,0:T(8,128)} copy(s32[16,3]{0,1:T(4,128)} %param.11) | data formatting | bytes 384 | tf_op args[1]
  2.3 0.7 copy_bitcast_fusion.pos
  3.0 97.2 %shard_map.100 = f32[2,96,128]{2,1,0:T(8,128)} custom-call(s32[16,3]{1,0:T(8,128)} %copy.12.tl_hbm, bf16[2,96,768]{2,1,0:T(8,128)(2,1)} %strip.1, bf16[4,16,1024]{2,1,0:T(8,128)(2,1)} %copy_bitcast_fusion.pos, bf16[2,96,1024]{2,1,0:T(8,128)(2,1)} %bitcast.12, bf16[2,32,1024]{2,1,0:T(8,128)(2,1)} %bitcast.13, f32[3,1024]{1,0:T(4,128)} %gains.1, ...), custom_call_target="tpu_custom_call" | custom-call | tf_op jit(solution)/shard_map/pallas_call | solution.py:579
  100.2 1.5 %copy.15 = f32[2,96,128]{2,1,0:T(8,128)} copy(f32[2,96,128]{2,1,0:T(8,128)} %shard_map.100) | data formatting | bytes 196608
Async XLA Ops:
  0.0 1.0 copy-start

commit v6 on v5

--- a/solution.py
+++ b/solution.py
@@ -103,8 +103,8 @@
     loop(1, N, greet)
 
     loads[4].wait()
-    owners = [tl[t, 0] for t in range(N)]
-    starts = [tl[t, 1] - tl[t, 2] for t in range(N)]
+    owners = [tl[0, t] for t in range(N)]
+    starts = [tl[1, t] - tl[2, t] for t in range(N)]
     ranks = []
     for t in range(N):
         rank = jnp.int32(0)
@@ -582,7 +582,7 @@
         in_specs=[hbm] + [vmem] * 5 + [hbm] * 4,
         out_specs=vmem,
         scratch_shapes=[
-            pltpu.SMEM((N, 3), jnp.int32),
+            pltpu.SMEM((3, N), jnp.int32),
             pltpu.VMEM((PV, D), bf),
             pltpu.VMEM((D, 3 * D), bf),
             pltpu.VMEM((D, D), bf),
@@ -621,7 +621,7 @@
             collective_id=0, has_side_effects=True, vmem_limit_bytes=56 * 1024 * 1024
         ),
     )(
-        tile_list, scene_band, pos, wq, wo, norm_gains,
+        tile_list.T, scene_band, pos, wq, wo, norm_gains,
         embed_weight, window_qkv, window_out, head_weight,
     )
 

time: 102 us -> 101 us (level)
  local copies, waits for them, and re-layouts: 4.5 us -> 3.15 us
    unnamed x4 -> x3, local copies, waits for them, and re-layouts: 3.85 us -> 2.49 us
where the time goes in v6:
time: 101 us; the launch traced here: 100 us
  Pallas kernels  97.2 us (96%)
  local copies, waits for them, and re-layouts  3.15 us (3%)
    pallas_call x1, Pallas kernels, local(): pl.pallas_call(kernel, out_shape=jax.ShapeDtypeStruct((2, SC, NCLS), jnp....  97.2 us
    unnamed x3, local copies, waits for them, and re-layouts  2.49 us

profile of v6, /device:TPU:1, one launch (start us, length us, event | category | flops | bytes accessed | tf_op | source)
XLA Modules:
  0.0 100.4 jit_solution(8798360518627876461)
XLA Ops:
  0.0 0.0 copy-start
  0.0 0.9 copy-done
  1.0 0.7 copy_bitcast_fusion.pos
  1.6 97.2 %shard_map.100 = f32[2,96,128]{2,1,0:T(8,128)} custom-call(s32[3,16]{1,0:T(4,128)} %bitcast.15, bf16[2,96,768]{2,1,0:T(8,128)(2,1)} %strip.1, bf16[4,16,1024]{2,1,0:T(8,128)(2,1)} %copy_bitcast_fusion.pos, bf16[2,96,1024]{2,1,0:T(8,128)(2,1)} %bitcast.13, bf16[2,32,1024]{2,1,0:T(8,128)(2,1)} %bitcast.14, f32[3,1024]{1,0:T(4,128)} %gains.1, ...), custom_call_target="tpu_custom_call" | custom-call | tf_op jit(solution)/shard_map/pallas_call | solution.py:579
  98.8 1.5 %copy.14 = f32[2,96,128]{2,1,0:T(8,128)} copy(f32[2,96,128]{2,1,0:T(8,128)} %shard_map.100) | data formatting | bytes 196608
Async XLA Ops:
  0.0 1.0 copy-start

commit v7 on v6

--- a/solution.py
+++ b/solution.py
@@ -369,12 +369,29 @@
     x_ref[...] = stream
     nall[x_at] = layer_norm(stream, gains[1:2])
 
-    def tokens_x(k):
-        at = nall.at[x_at]
-        return remote(at, at, ns.at[k - 1], nr.at[x_at], i, ((x_at + k) % 4) * 4 + z_at)
-
-    for k in (1, 3, 2):
-        tokens_x(k).start()
+    def tokens_at(x, part):
+        if part == 2:
+            return nall.at[x % 4]
+        return nall.at[x % 4, pl.ds(part * 64, 64)]
+
+    def tokens_x(step, part, x, number):
+        at = tokens_at(x, part)
+        return remote(
+            at, at, ns.at[number], nr.at[part, x % 4], i, ((x_at + step) % 4) * 4 + z_at
+        )
+
+    def tokens_in(x, part):
+        at = tokens_at(x, part)
+        remote(at, at, ns.at[0], nr.at[part, x % 4], i, r).wait_recv()
+
+    tokens_copies = [
+        tokens_x(1, 2, x_at, 0),
+        tokens_x(3, 2, x_at, 1),
+        tokens_x(1, 0, x_at + 3, 2),
+        tokens_x(3, 1, x_at + 1, 3),
+    ]
+    tokens_copies[0].start()
+    tokens_copies[1].start()
     pass_weights_last()
     for k in range(1, 4):
         z = (z_at + k) % 4
@@ -391,9 +408,14 @@
 
     for step in (0, 1, 3, 2):
         x = (x_at + step) % 4
-        if step > 0:
-            at = nall.at[x]
-            remote(at, at, ns.at[0], nr.at[x], i, r).wait_recv()
+        if step == 1:
+            tokens_in(x_at + 3, 2)
+            tokens_copies[2].start()
+            tokens_in(x_at + 1, 2)
+            tokens_copies[3].start()
+        elif step == 2:
+            tokens_in(x_at + 2, 0)
+            tokens_in(x_at + 2, 1)
         tokens = nall[x]
         for k in (1, 2, 3, 0):
             quarter = (fourth + k) % 4
@@ -542,8 +564,7 @@
     sib.wait_send()
     for k in range(1, 4):
         weights_sibling(k).wait_send()
-        tokens_x(k).wait_send()
-    for copy in weights_copies:
+    for copy in weights_copies + tokens_copies:
         copy.wait_send()
     out_sent()
 
@@ -611,7 +632,7 @@
             pltpu.VMEM((N, MOST, 16, NCLS), bf),
             pltpu.VMEM((4, 128, D), bf),
             pltpu.SemaphoreType.REGULAR,
-            dma((3,)), dma((4,)),
+            dma((4,)), dma((3, 4)),
             dma((N,)), dma((N,)), dma((N,)), dma((N,)), dma((8,)), dma((8,)), dma, dma,
             dma((4,)), dma((4,)), dma((3, 4)), dma((4,)),
             dma((3,)), dma((3,)), dma((3,)), dma((3,)), dma((4,)), dma((4,)), dma((4,)), dma((4,)),

time: 101 us -> 98.8 us (0.978)
  Pallas kernels: 97.2 us -> 95.5 us
    pallas_call x1, Pallas kernels: 97.2 us -> 95.5 us  [local(): pl.pallas_call(kernel, out_shape=jax.ShapeDtypeStruct((2, SC, NCLS), jnp....]
where the time goes in v7:
time: 98.8 us; the launch traced here: 98.6 us
  Pallas kernels  95.5 us (97%)
  local copies, waits for them, and re-layouts  3.15 us (3%)
    pallas_call x1, Pallas kernels, local(): pl.pallas_call(kernel, out_shape=jax.ShapeDtypeStruct((2, SC, NCLS), jnp....  95.5 us
    unnamed x3, local copies, waits for them, and re-layouts  2.49 us

profile of v7, /device:TPU:1, one launch (start us, length us, event | category | flops | bytes accessed | tf_op | source)
XLA Modules:
  0.0 98.6 jit_solution(3365071345372005643)
XLA Ops:
  0.0 0.0 copy-start
  0.0 0.9 copy-done
  1.0 0.7 copy_bitcast_fusion.pos
  1.6 95.5 %shard_map.100 = f32[2,96,128]{2,1,0:T(8,128)} custom-call(s32[3,16]{1,0:T(4,128)} %bitcast.15, bf16[2,96,768]{2,1,0:T(8,128)(2,1)} %strip.1, bf16[4,16,1024]{2,1,0:T(8,128)(2,1)} %copy_bitcast_fusion.pos, bf16[2,96,1024]{2,1,0:T(8,128)(2,1)} %bitcast.13, bf16[2,32,1024]{2,1,0:T(8,128)(2,1)} %bitcast.14, f32[3,1024]{1,0:T(4,128)} %gains.1, ...), custom_call_target="tpu_custom_call" | custom-call | tf_op jit(solution)/shard_map/pallas_call | solution.py:600
  97.1 1.5 %copy.14 = f32[2,96,128]{2,1,0:T(8,128)} copy(f32[2,96,128]{2,1,0:T(8,128)} %shard_map.100) | data formatting | bytes 196608
Async XLA Ops:
  0.0 1.0 copy-start
